TPU v7x, 32 devices: a whole 2x2x4 slice. The times are simulated.
32 devices in a mesh: section: 4 (over y, x), dp: 8 (over z, core).
Axes of the slice: x: 2, y: 2, z: 4, core: 2. Of those that a mesh axis runs over, the one named last changes fastest.
Arguments:
- inputs: bfloat16 [4, 1024, 512], P('section', 'dp'), may hold values from -6 to 6
- cotangent: bfloat16 [4, 1024, 512], P('section', 'dp'), may hold values from -6 to 6
- section_weights: bfloat16 [2048, 4096], P('section')
- norm_gains: float32 [2048], P('section'), may hold values from 0.5 to 1.5
- doc_lengths: int32 [4, 8, 6], P('section', 'dp'), may hold values from 1 to 64, 128 in all within a row
- slot_fill: int32 [4, 8], P('section', 'dp'), may hold values from 96 to 128, as said below
Outputs:
- input_grad: bfloat16 [4, 1024, 512], P('section', 'dp')
- weight_grads: float32 [2048, 4096], P('section')
- gain_grads: float32 [2048], P('section')
- forget_mean: float32 [2], replicated
Inputs may be any that keep to these rules, and one draw needn't show every extreme that they name: `slot_fill`: every slot is filled from its start; some slot of every draw is full. `doc_lengths`: the lengths of a slot's documents add up to 128.
All inputs are finite; a program needn't handle non-finite values.
Results may differ from a plain program's by a relative error of at most 0.01.
Values may be sent and summed in bfloat16 or wider, within the bound.
A program may use at most 320 MiB of HBM per device.

v0:
```python
import jax
import jax.numpy as jnp
from jax import lax
from jax.sharding import PartitionSpec as P

EPS = 1e-06


def shortened(shard):
    return jax.tree.map(lambda a: a.astype(jnp.bfloat16) if a.dtype == jnp.float32 else a, shard)


def from_behind(shard, axis, by):
    length = lax.axis_size(axis)
    pairs = [(i, i + by) for i in range(length) if 0 <= i + by < length]
    return lax.ppermute(shard, axis, pairs)


def rms_norm(values, norm_gain):
    return values * lax.rsqrt(jnp.mean(values * values, axis=-1, keepdims=True) + EPS) * norm_gain


def mix_gates(projection, keep_mask):
    width = projection.shape[1] // 3
    gate_gap = jax.nn.softplus(-projection[:, :width]) - jax.nn.softplus(
        -projection[:, width : 2 * width]
    )
    forget = jnp.exp(-jax.nn.softplus(gate_gap))
    drive_term = jnp.exp(-jax.nn.softplus(-gate_gap)) * jax.nn.softplus(projection[:, 2 * width :])
    return (forget * keep_mask[:, None], drive_term, forget)


def combine(earlier, later):
    return (earlier[0] * later[0], later[0] * earlier[1] + later[1])


def recurrence(decay_rate, drive_term):
    return lax.associative_scan(combine, (decay_rate, drive_term), axis=0)[1]


def contract_rows(left, right):
    return lax.dot_general(
        left, right, (((0,), (0,)), ((), ())), preferred_element_type=jnp.float32
    )


def contract_cols(left, right):
    return lax.dot_general(
        left, right, (((1,), (1,)), ((), ())), preferred_element_type=jnp.float32
    )


def weight_rows(left_first, left_second, right_side, split):
    return jnp.concatenate(
        [
            contract_rows(left_first, right_side[:, :split]),
            contract_rows(left_second, right_side[:, split:]),
        ],
        1,
    )


def mixer_forward(residual, norm_gain, weight_block, keep_mask):
    width = weight_block.shape[1] // 4
    normed = rms_norm(residual, norm_gain).astype(jnp.bfloat16)
    projection = jnp.dot(normed, weight_block[:, : 3 * width], preferred_element_type=jnp.float32)
    decay_rate, drive_term, forget = mix_gates(projection, keep_mask)
    hidden_state = recurrence(decay_rate, drive_term).astype(jnp.bfloat16)
    return (residual + contract_cols(hidden_state, weight_block[:, 3 * width :]), forget)


def feed_forward(residual, norm_gain, weight_block):
    width = weight_block.shape[1] // 2
    normed = rms_norm(residual, norm_gain).astype(jnp.bfloat16)
    hidden_units = jnp.dot(normed, weight_block[:, :width], preferred_element_type=jnp.float32)
    activated = jax.nn.gelu(hidden_units, approximate=False).astype(jnp.bfloat16)
    return residual + contract_cols(activated, weight_block[:, width:])


def mixer_backward(residual, norm_gain, weight_block, keep_mask, grad_out):
    width = weight_block.shape[1] // 4
    w_in = weight_block[:, : 3 * width]
    w_out = weight_block[:, 3 * width :]
    normed, norm_pull = jax.vjp(rms_norm, residual, norm_gain)
    normed_low = normed.astype(jnp.bfloat16)
    projection = jnp.dot(normed_low, w_in, preferred_element_type=jnp.float32)
    (decay_rate, drive_term), gate_pull = jax.vjp(
        lambda values: mix_gates(values, keep_mask)[:2], projection
    )
    hidden_state = recurrence(decay_rate, drive_term)
    grad_low = grad_out.astype(jnp.bfloat16)
    d_state = jnp.dot(grad_low, w_out, preferred_element_type=jnp.float32)
    next_decay = jnp.concatenate([decay_rate[1:], jnp.zeros_like(decay_rate[:1])], 0)
    adjoint = jnp.flip(recurrence(jnp.flip(next_decay, 0), jnp.flip(d_state, 0)), 0)
    previous = jnp.concatenate([jnp.zeros_like(hidden_state[:1]), hidden_state[:-1]], 0)
    (d_projection,) = gate_pull((adjoint * previous, adjoint))
    d_projection_low = d_projection.astype(jnp.bfloat16)
    d_normed = contract_cols(d_projection_low, w_in)
    d_residual, d_gain = norm_pull(d_normed)
    right_side = jnp.concatenate([d_projection_low, hidden_state.astype(jnp.bfloat16)], 1)
    return (grad_out + d_residual, d_gain, normed_low, grad_low, right_side)


def feed_backward(residual, norm_gain, weight_block, grad_out):
    width = weight_block.shape[1] // 2
    w_up = weight_block[:, :width]
    w_down = weight_block[:, width:]
    normed, norm_pull = jax.vjp(rms_norm, residual, norm_gain)
    normed_low = normed.astype(jnp.bfloat16)
    hidden_units = jnp.dot(normed_low, w_up, preferred_element_type=jnp.float32)
    activated, act_pull = jax.vjp(
        lambda values: jax.nn.gelu(values, approximate=False), hidden_units
    )
    grad_low = grad_out.astype(jnp.bfloat16)
    d_activated = jnp.dot(grad_low, w_down, preferred_element_type=jnp.float32)
    (d_hidden,) = act_pull(d_activated)
    d_hidden_low = d_hidden.astype(jnp.bfloat16)
    d_normed = contract_cols(d_hidden_low, w_up)
    d_residual, d_gain = norm_pull(d_normed)
    right_side = jnp.concatenate([d_hidden_low, activated.astype(jnp.bfloat16)], 1)
    return (grad_out + d_residual, d_gain, normed_low, grad_low, right_side)


def pick_micro(stack, position):
    return lax.dynamic_index_in_dim(stack, position, 0, keepdims=False)


def local(inputs, cotangent, section_weights, norm_gains, doc_lengths, slot_fill):
    section_index = lax.axis_index("section")
    section_count = lax.axis_size("section")
    slot_length = inputs.shape[1]
    model_width = inputs.shape[2]
    pack_width = section_weights.shape[1]
    gate_width = pack_width // 4
    positions = jnp.arange(slot_length, dtype=jnp.int32)
    lengths = doc_lengths[0, 0]
    starts = jnp.cumsum(lengths) - lengths
    keep_own = 1.0 - jnp.any(positions[:, None] == starts[None, :], axis=1).astype(jnp.float32)
    valid_own = (positions < slot_fill[0, 0]).astype(jnp.float32)
    all_inputs, all_cotangents, all_keeps, all_valids = (
        lax.all_gather(inputs, "section", axis=0, tiled=True),
        lax.all_gather(cotangent, "section", axis=0, tiled=True),
        lax.all_gather(keep_own[None].astype(jnp.bfloat16), "section", axis=0, tiled=True),
        lax.all_gather(valid_own[None].astype(jnp.bfloat16), "section", axis=0, tiled=True),
    )
    micro_count = all_inputs.shape[0]
    tick_count = micro_count + section_count - 1
    section_kind = 1 + section_index % 2

    def spare_forward(section_input, keep_mask, valid_mask):
        return (jnp.zeros_like(section_input), jnp.zeros((), jnp.float32))

    def mixer_branch(section_input, keep_mask, valid_mask):
        result, forget = mixer_forward(
            section_input.astype(jnp.float32), norm_gains, section_weights, keep_mask
        )
        return (result.astype(jnp.bfloat16), jnp.sum(forget * valid_mask[:, None]))

    def dense_branch(section_input, keep_mask, valid_mask):
        result = feed_forward(section_input.astype(jnp.float32), norm_gains, section_weights)
        return (result.astype(jnp.bfloat16), jnp.zeros((), jnp.float32))

    received = jnp.zeros_like(inputs[0])
    kept_inputs = jnp.zeros_like(all_inputs)
    forget_total = jnp.zeros((), jnp.float32)
    for step_index in range(tick_count):
        micro_index = step_index - section_index
        is_active = (micro_index >= 0) & (micro_index < micro_count)
        micro_clip = jnp.clip(micro_index, 0, micro_count - 1)
        section_input = jnp.where(section_index == 0, pick_micro(all_inputs, micro_clip), received)
        kept_inputs = lax.dynamic_update_index_in_dim(
            kept_inputs,
            jnp.where(is_active, section_input, pick_micro(kept_inputs, micro_clip)),
            micro_clip,
            0,
        )
        branch_pick = jnp.where(is_active & (section_index < section_count - 1), section_kind, 0)
        section_output, forget_part = lax.switch(
            branch_pick,
            [spare_forward, mixer_branch, dense_branch],
            section_input,
            pick_micro(all_keeps, micro_clip).astype(jnp.float32),
            pick_micro(all_valids, micro_clip).astype(jnp.float32),
        )
        forget_total = forget_total + forget_part
        if step_index < tick_count - 1:
            received = jax.tree.map(
                lambda part, own: part.astype(own.dtype),
                from_behind(shortened(section_output), "section", 1),
                section_output,
            )
    forget_vector = jnp.stack(
        [
            jnp.where(section_index == 0, forget_total, 0.0),
            jnp.where(section_index == 2, forget_total, 0.0),
        ]
    )
    valid_count = jnp.sum(valid_own)
    forget_sums, count_sum = lax.psum((forget_vector, valid_count), ("section", "dp"))

    def spare_backward(section_input, keep_mask, grad_out):
        return (
            jnp.zeros_like(grad_out),
            jnp.zeros(norm_gains.shape, jnp.float32),
            jnp.zeros(section_input.shape, jnp.bfloat16),
            jnp.zeros(section_input.shape, jnp.bfloat16),
            jnp.zeros((section_input.shape[0], pack_width), jnp.bfloat16),
        )

    def mixer_back_branch(section_input, keep_mask, grad_out):
        return mixer_backward(
            section_input.astype(jnp.float32), norm_gains, section_weights, keep_mask, grad_out
        )

    def dense_back_branch(section_input, keep_mask, grad_out):
        return feed_backward(
            section_input.astype(jnp.float32), norm_gains, section_weights, grad_out
        )

    def mixer_rows(left_first, left_second, right_side):
        return weight_rows(left_first, left_second, right_side, 3 * gate_width)

    def dense_rows(left_first, left_second, right_side):
        return weight_rows(left_first, left_second, right_side, pack_width // 2)

    grad_received = jnp.zeros_like(inputs[0])
    weight_total = jnp.zeros(section_weights.shape, jnp.float32)
    gain_total = jnp.zeros(norm_gains.shape, jnp.float32)
    grad_store = jnp.zeros_like(all_inputs)
    for step_index in range(tick_count):
        micro_index = step_index - (section_count - 1 - section_index)
        is_active = (micro_index >= 0) & (micro_index < micro_count)
        micro_clip = jnp.clip(micro_index, 0, micro_count - 1)
        valid_mask = pick_micro(all_valids, micro_clip).astype(jnp.float32)
        seed_grad = pick_micro(all_cotangents, micro_clip).astype(jnp.float32) * valid_mask[:, None]
        grad_out = jnp.where(
            section_index == section_count - 1, seed_grad, grad_received.astype(jnp.float32)
        )
        branch_pick = jnp.where(is_active, section_kind, 0)
        grad_in, gain_part, normed_low, outgrad_low, right_side = lax.switch(
            branch_pick,
            [spare_backward, mixer_back_branch, dense_back_branch],
            pick_micro(kept_inputs, micro_clip),
            pick_micro(all_keeps, micro_clip).astype(jnp.float32),
            grad_out,
        )
        gain_total = gain_total + gain_part
        weight_total = weight_total + lax.switch(
            section_kind - 1, [mixer_rows, dense_rows], normed_low, outgrad_low, right_side
        )
        grad_low = grad_in.astype(jnp.bfloat16)
        grad_store = lax.dynamic_update_index_in_dim(
            grad_store,
            jnp.where(is_active, grad_low, pick_micro(grad_store, micro_clip)),
            micro_clip,
            0,
        )
        if step_index < tick_count - 1:
            grad_received = from_behind(grad_low, "section", -1)
    weight_grads, gain_sums = lax.psum((weight_total, gain_total), "dp")
    gain_grads = gain_sums[:model_width]
    forget_mean = forget_sums / (count_sum * gate_width)
    returned = grad_store[0]
    for micro_number in range(1, micro_count):
        arrived = from_behind(grad_store[micro_number], "section", micro_number)
        returned = jnp.where(section_index == micro_number, arrived, returned)
    return (returned[None], weight_grads, gain_grads, forget_mean)


def solution(mesh):
    placed = (
        P("section", "dp", None),
        P("section", "dp", None),
        P("section", None),
        P("section"),
        P("section", "dp", None),
        P("section", "dp"),
    )
    return jax.shard_map(
        local,
        mesh=mesh,
        in_specs=placed,
        out_specs=(P("section", "dp", None), P("section", None), P("section"), P()),
        check_vma=False,
    )
```

profile of v0, /device:TPU:0, one launch (start us, length us, event | category | flops | bytes accessed | tf_op | source)
XLA Modules:
  0.0 1072.3 jit_solution(17594064218336927256)
XLA Ops:
  9.5 9.4 all-gather.2
  18.9 7.9 all-gather.1
  26.8 10.5 all_gather.12
  37.4 10.8 %conditional.21 = (bf16[128,512]{1,0:T(8,128)(2,1)S(1)}, f32[]{:T(128)}) conditional(s32[]{:T(128)} %clamp.52, () %tuple.280, (bf16[128,512]{1,0:T(8,128)(2,1)S(1)}, f32[512]{0:T(512)}, bf16[512,4096]{1,0:T(8,128)(2,1)}, bf16[4,128]{1,0:T(4,128)(2,1)S(1)}, s32[]{:T(128)}, /*index=5*/bf16[4,128]{1,0:T(4,128)(2,1)S(1)}) %tuple.732, ...), branch_computations={%region_2.3_spmd, %region_3.6_spmd, %region_6.8_spmd} | conditional | flops 554565760 | bytes 28375624 | solution.py:178
  52.0 11.3 %conditional.22 = (bf16[128,512]{1,0:T(8,128)(2,1)S(1)}, f32[]{:T(128)}) conditional(s32[]{:T(128)} %clamp.53, () %tuple.283, (bf16[128,512]{1,0:T(8,128)(2,1)S(1)}, f32[512]{0:T(512)}, bf16[512,4096]{1,0:T(8,128)(2,1)}, bf16[4,128]{1,0:T(4,128)(2,1)S(1)}, s32[]{:T(128)}, /*index=5*/bf16[4,128]{1,0:T(4,128)(2,1)S(1)}) %tuple.733, ...), branch_computations={%region_8.9_spmd, %region_9.12_spmd, %region_12.14_spmd} | conditional | flops 554565760 | bytes 28375624 | solution.py:178
  67.2 10.9 %conditional.23 = (bf16[128,512]{1,0:T(8,128)(2,1)S(1)}, f32[]{:T(128)}) conditional(s32[]{:T(128)} %clamp.54, () %tuple.286, (bf16[128,512]{1,0:T(8,128)(2,1)S(1)}, f32[512]{0:T(512)}, bf16[512,4096]{1,0:T(8,128)(2,1)}, bf16[4,128]{1,0:T(4,128)(2,1)S(1)}, s32[]{:T(128)}, /*index=5*/bf16[4,128]{1,0:T(4,128)(2,1)S(1)}) %tuple.734, ...), branch_computations={%region_14.15_spmd, %region_15.18_spmd, %region_18.20_spmd} | conditional | flops 554565760 | bytes 28375624 | solution.py:178
  81.9 11.5 %conditional.24 = (bf16[128,512]{1,0:T(8,128)(2,1)S(1)}, f32[]{:T(128)}) conditional(s32[]{:T(128)} %clamp.55, () %tuple.289, (bf16[128,512]{1,0:T(8,128)(2,1)S(1)}, f32[512]{0:T(512)}, bf16[512,4096]{1,0:T(8,128)(2,1)}, bf16[4,128]{1,0:T(4,128)(2,1)S(1)}, s32[]{:T(128)}, /*index=5*/bf16[4,128]{1,0:T(4,128)(2,1)S(1)}) %tuple.735, ...), branch_computations={%region_20.21_spmd, %region_21.24_spmd, %region_24.26_spmd} | conditional | flops 554565760 | bytes 28375624 | solution.py:178
  97.4 14.0 %collective-permute-start.4 = (bf16[128,512]{1,0:T(8,128)(2,1)S(1)}, bf16[128,512]{1,0:T(8,128)(2,1)S(1)}, u32[]{:S(2)}, u32[]{:S(2)}) collective-permute-start(bf16[128,512]{1,0:T(8,128)(2,1)S(1)} %get-tuple-element.1018), channel_id=1, source_target_pairs={{0,8},{8,16},{16,24},{1,9},{9,17},{17,25},{2,10},{10,18},{18,26},{... | collective-permute-start | bytes 393224 | tf_op jit(solution)/shard_map/ppermute | solution.py:16
  111.4 17.0 %all_gather.15 = bf16[4,128,512]{2,1,0:T(8,128)(2,1)S(1)} all-gather(bf16[1,128,512]{2,1,0:T(8,128)(2,1)S(1)} %copy-done.111), channel_id=1, replica_groups=mesh['section'=4,'dp'=8] {'section'}, dimensions={0}, use_global_device_ids=true | all-gather | bytes 655360 | tf_op jit(solution)/shard_map/all_gather | solution.py:142
  128.5 9.3 conditional.26
  144.1 11.3 %conditional.27 = (f32[512]{0:T(512)}, bf16[128,512]{1,0:T(8,128)(2,1)}, bf16[128,512]{1,0:T(8,128)(2,1)}, bf16[128,4096]{1,0:T(8,128)(2,1)S(1)}, bf16[128,512]{1,0:T(8,128)(2,1)}) conditional(s32[]{:T(128)} %clamp.51, () %tuple.279, (bf16[128,512]{1,0:T(8,128)(2,1)S(1)}, f32[512]{0:T(512)}, bf16[512,4096]{1,0:T(8,128)(2,1)}, ...), branch_computations={%region_38.39_spmd, %region_39.44_spmd, %region_43.48_spmd} | conditional | flops 962065792 | bytes 94740368 | solution.py:240
  156.7 9.3 collective-permute-done.6
  167.0 12.1 %conditional.28 = (f32[512]{0:T(512)}, bf16[128,512]{1,0:T(8,128)(2,1)}, bf16[128,512]{1,0:T(8,128)(2,1)}, bf16[128,4096]{1,0:T(8,128)(2,1)}, bf16[128,512]{1,0:T(8,128)(2,1)}) conditional(s32[]{:T(128)} %clamp.58, () %tuple.300, (bf16[128,512]{1,0:T(8,128)(2,1)S(1)}, f32[512]{0:T(512)}, bf16[512,4096]{1,0:T(8,128)(2,1)}, ...), branch_computations={%region_47.49_spmd, %region_48.53_spmd, %region_52.57_spmd} | conditional | flops 962065792 | bytes 99049312 | solution.py:240
  180.4 7.0 collective-permute-done.7
  188.4 11.3 %conditional.29 = (f32[512]{0:T(512)}, bf16[128,512]{1,0:T(8,128)(2,1)}, bf16[128,512]{1,0:T(8,128)(2,1)}, bf16[128,4096]{1,0:T(8,128)(2,1)S(1)}, bf16[128,512]{1,0:T(8,128)(2,1)}) conditional(s32[]{:T(128)} %clamp.59, () %tuple.303, (bf16[128,512]{1,0:T(8,128)(2,1)S(1)}, f32[512]{0:T(512)}, bf16[512,4096]{1,0:T(8,128)(2,1)}, ...), branch_computations={%region_56.58_spmd, %region_57.62_spmd, %region_61.66_spmd} | conditional | flops 962065792 | bytes 95362912 | solution.py:240
  201.0 77.3 %collective-permute-done.8 = bf16[128,512]{1,0:T(8,128)(2,1)S(1)} collective-permute-done((bf16[128,512]{1,0:T(8,128)(2,1)}, bf16[128,512]{1,0:T(8,128)(2,1)S(1)}, u32[]{:S(2)}, u32[]{:S(2)}) %collective-permute-start.8) | collective-permute-done | bytes 131104 | tf_op jit(solution)/shard_map/ppermute | solution.py:16
  279.3 75.8 %conditional.30 = (f32[512]{0:T(512)}, bf16[128,512]{1,0:T(8,128)(2,1)}, bf16[128,512]{1,0:T(8,128)(2,1)}, bf16[128,4096]{1,0:T(8,128)(2,1)}, bf16[128,512]{1,0:T(8,128)(2,1)}) conditional(s32[]{:T(128)} %clamp.60, () %tuple.306, (bf16[128,512]{1,0:T(8,128)(2,1)S(1)}, f32[512]{0:T(512)}, bf16[512,4096]{1,0:T(8,128)(2,1)}, ...), branch_computations={%region_65.67_spmd, %region_66.71_spmd, %region_70.75_spmd} | conditional | flops 962065792 | bytes 100081536 | solution.py:240
  283.3 2.6 slice.4729
  328.0 2.7 pad.1224
  334.5 4.7 rev.39
  339.2 3.2 fusion.1128
  356.5 54.5 %collective-permute-done.9 = bf16[128,512]{1,0:T(8,128)(2,1)S(1)} collective-permute-done((bf16[128,512]{1,0:T(8,128)(2,1)}, bf16[128,512]{1,0:T(8,128)(2,1)S(1)}, u32[]{:S(2)}, u32[]{:S(2)}) %collective-permute-start.9) | collective-permute-done | bytes 131104 | tf_op jit(solution)/shard_map/ppermute | solution.py:16
  412.0 102.7 %conditional.31 = (f32[512]{0:T(512)}, bf16[128,512]{1,0:T(8,128)(2,1)}, bf16[128,512]{1,0:T(8,128)(2,1)}, bf16[128,4096]{1,0:T(8,128)(2,1)S(1)}, bf16[128,512]{1,0:T(8,128)(2,1)}) conditional(s32[]{:T(128)} %clamp.61, () %tuple.309, (bf16[128,512]{1,0:T(8,128)(2,1)S(1)}, f32[512]{0:T(512)}, bf16[512,4096]{1,0:T(8,128)(2,1)}, ...), branch_computations={%region_74.76_spmd, %region_75.80_spmd, %region_79.84_spmd} | conditional | flops 962065792 | bytes 93789968 | solution.py:240
  460.5 2.6 pad.1271
  473.3 2.6 slice.4792
  489.9 2.6 pad.1256
  494.6 4.8 rev.40
  499.4 3.2 fusion.1183
  516.0 5.8 collective-permute-done.10
  522.9 194.1 %conditional.32 = (f32[512]{0:T(512)}, bf16[128,512]{1,0:T(8,128)(2,1)}, bf16[128,512]{1,0:T(8,128)(2,1)}, bf16[128,4096]{1,0:T(8,128)(2,1)}, bf16[128,512]{1,0:T(8,128)(2,1)}) conditional(s32[]{:T(128)} %clamp.62, () %tuple.312, (bf16[128,512]{1,0:T(8,128)(2,1)S(1)}, f32[512]{0:T(512)}, bf16[512,4096]{1,0:T(8,128)(2,1)}, ...), branch_computations={%region_83.85_spmd, %region_84.89_spmd, %region_88.93_spmd} | conditional | flops 962065792 | bytes 95281072 | solution.py:240
  528.3 2.6 slice.4963
  637.8 2.6 pad.1302
  689.3 2.6 pad.1286
  692.0 2.6 pad.1287
  696.6 4.7 rev.41
  701.4 3.3 fusion.1238
  718.3 10.5 conditional.34
  718.3 2.7 fusion.883
  723.0 5.8 pad_maximum_fusion.43
  728.8 7.7 conditional.35
  732.5 4.1 pad_maximum_fusion.45
  736.6 6.6 conditional.36
  739.0 4.1 pad_maximum_fusion.47
  743.1 8.0 conditional.37
  746.9 4.2 pad_maximum_fusion.49
  751.1 6.5 conditional.38
  753.5 4.1 pad_maximum_fusion.51
  757.6 8.0 conditional.39
  761.4 4.3 pad_maximum_fusion.53
  766.7 79.7 %conditional.33 = (f32[512]{0:T(512)}, bf16[128,512]{1,0:T(8,128)(2,1)}, bf16[128,512]{1,0:T(8,128)(2,1)}, bf16[128,4096]{1,0:T(8,128)(2,1)S(1)}, bf16[128,512]{1,0:T(8,128)(2,1)}) conditional(s32[]{:T(128)} %clamp.63, () %tuple.315, (bf16[128,512]{1,0:T(8,128)(2,1)S(1)}, f32[512]{0:T(512)S(1)}, bf16[512,4096]{1,0:T(8,128)(2,1)}, ...), branch_computations={%region_92.94_spmd, %region_93.98_spmd, %region_97.102_spmd} | conditional | flops 962065792 | bytes 95354672 | solution.py:240
  769.4 2.6 slice.5080
  819.8 2.6 slice.5026
  830.6 2.6 pad.1318
  835.1 4.7 rev.42
  839.8 3.2 fusion.1293
  846.5 10.6 conditional.40
  846.5 2.7 fusion.931
  851.1 6.0 pad_maximum_fusion.55
  857.0 23.8 %add_add_fusion.14 = f32[512,4096]{1,0:T(8,128)} fusion(f32[512,4096]{1,0:T(8,128)} %get-tuple-element.1659, f32[512,4096]{1,0:T(8,128)} %get-tuple-element.1658, f32[512,4096]{1,0:T(8,128)} %get-tuple-element.1657, f32[512,4096]{1,0:T(8,128)} %get-tuple-element.1656, f32[512,4096]{1,0:T(8,128)} %get-tuple-element.1655, ...), kind=kLoop, calls=%fused_computation.2243 | loop fusion | flops 12582912 | bytes 67108864 | tf_op jit(solution)/shard_map/add | solution.py:248
  881.8 41.2 %all-reduce.315 = (f32[2]{0:T(128)S(1)}, f32[]{:T(128)}) all-reduce(f32[2]{0:T(128)S(1)} %pad_maximum_fusion.148, f32[]{:T(128)} %fusion.1350), channel_id=1, replica_groups=mesh['section'=4,'dp'=8] {'section','dp'}, use_global_device_ids=true, to_apply=%region_122.124 | all-reduce | flops 3 | bytes 24 | tf_op jit(solution)/shard_map/psum | solution.py:199
  928.4 4.2 collective-permute-start.14
  936.7 16.0 %psum.29 = f32[512]{0:T(512)} all-reduce(f32[512]{0:T(512)S(1)} %add_add_fusion.15), channel_id=1, replica_groups=mesh['section'=4,'dp'=8] {'dp'}, use_global_device_ids=true, to_apply=%region_116.118 | all-reduce | flops 512 | bytes 4096 | tf_op jit(solution)/shard_map/psum | solution.py:260
  953.4 103.9 %all-reduce.318.cloned.1.call-done = f32[512,4096]{1,0:T(8,128)} async-done(((f32[512,4096]{1,0:T(8,128)}), f32[512,4096]{1,0:T(8,128)}) %all-reduce.318.cloned.1.call-update) | async-done | bytes 8388624 | tf_op jit(solution)/shard_map/psum | solution.py:260
  1057.3 7.8 copy.218
  (1310 shorter events, 476.4 us)
Async XLA Ops:
  7.2 1050.1 %all-reduce.318.cloned.1.call-start = ((), (), s32[]{:S(2)}) async-start(), calls=%async_computation | async-start | bytes 16777216 | tf_op jit(solution)/shard_map/psum | solution.py:260
  18.9 109.6 %copy-start.117 = (bf16[4,1,128]{2,0,1:T(4,128)(2,1)}, bf16[4,1,128]{2,0,1:T(4,128)(2,1)S(1)}, u32[]{:S(2)}) copy-start(bf16[4,1,128]{2,0,1:T(4,128)(2,1)S(1)} %copy.14) | copy-start | bytes 3076
  26.8 117.3 %copy-start.119 = (bf16[4,1,128]{2,0,1:T(4,128)(2,1)}, bf16[4,1,128]{2,0,1:T(4,128)(2,1)S(1)}, u32[]{:S(2)}) copy-start(bf16[4,1,128]{2,0,1:T(4,128)(2,1)S(1)} %copy.15) | copy-start | bytes 3076
  48.2 3.8 collective-permute-start
  63.3 3.8 collective-permute-start.1
  78.1 3.8 collective-permute-start.2
  93.4 3.8 collective-permute-start.3
  97.3 14.1 %copy-start.111 = (bf16[1,128,512]{2,1,0:T(8,128)(2,1)S(1)}, bf16[1,128,512]{2,1,0:T(8,128)(2,1)}, u32[]{:S(2)}) copy-start(bf16[1,128,512]{2,1,0:T(8,128)(2,1)} %param.64) | copy-start | bytes 393220
  97.4 31.0 %collective-permute-start.4 = (bf16[128,512]{1,0:T(8,128)(2,1)S(1)}, bf16[128,512]{1,0:T(8,128)(2,1)S(1)}, u32[]{:S(2)}, u32[]{:S(2)}) collective-permute-start(bf16[128,512]{1,0:T(8,128)(2,1)S(1)} %get-tuple-element.1018), channel_id=1, source_target_pairs={{0,8},{8,16},{16,24},{1,9},{9,17},{17,25},{2,10},{10,18},{18,26},{... | collective-permute-start | bytes 393224 | tf_op jit(solution)/shard_map/ppermute | solution.py:16
  128.4 11.4 %copy-start.25 = (bf16[4,128,512]{2,1,0:T(8,128)(2,1)}, bf16[4,128,512]{2,1,0:T(8,128)(2,1)S(1)}, u32[]{:S(2)}) copy-start(bf16[4,128,512]{2,1,0:T(8,128)(2,1)S(1)} %all_gather.15) | copy-start | bytes 1572868
  137.8 4.8 collective-permute-start.5
  155.4 11.6 %copy-start.14 = (bf16[128,4096]{1,0:T(8,128)(2,1)}, bf16[128,4096]{1,0:T(8,128)(2,1)S(1)}, u32[]{:S(2)}) copy-start(bf16[128,4096]{1,0:T(8,128)(2,1)S(1)} %get-tuple-element.1027) | copy-start | bytes 3145732
  155.4 10.6 collective-permute-start.6
  179.1 8.3 collective-permute-start.7
  199.7 79.6 %copy-start.16 = (bf16[128,4096]{1,0:T(8,128)(2,1)}, bf16[128,4096]{1,0:T(8,128)(2,1)S(1)}, u32[]{:S(2)}) copy-start(bf16[128,4096]{1,0:T(8,128)(2,1)S(1)} %get-tuple-element.1033) | copy-start | bytes 3145732
  199.7 78.6 %collective-permute-start.8 = (bf16[128,512]{1,0:T(8,128)(2,1)}, bf16[128,512]{1,0:T(8,128)(2,1)S(1)}, u32[]{:S(2)}, u32[]{:S(2)}) collective-permute-start(bf16[128,512]{1,0:T(8,128)(2,1)} %get-tuple-element.1022), channel_id=1, source_target_pairs={{8,0},{16,8},{24,16},{9,1},{17,9},{25,17},{10,2},{18,10},{26,18},{... | collective-permute-start | bytes 393224 | tf_op jit(solution)/shard_map/ppermute | solution.py:16
  280.1 21.0 %copy-start.141 = (f32[128]{0:T(128)}, f32[128]{0:T(128)S(1)}, u32[]{:S(2)}) copy-start(f32[128]{0:T(128)S(1)} %bitcast_convert_fusion.4) | copy-start | bytes 1540 | tf_op jit(solution)/shard_map/cond
  281.5 12.2 %copy-start.34 = (bf16[128,512]{1,0:T(8,128)(2,1)}, bf16[128,512]{1,0:T(8,128)(2,1)S(1)}, u32[]{:S(2)}) copy-start(bf16[128,512]{1,0:T(8,128)(2,1)S(1)} %fusion.1146) | copy-start | bytes 393220 | tf_op jit(solution)/shard_map/cond
  281.5 12.2 %copy-start.75 = (bf16[128,512]{1,0:T(8,128)(2,1)}, bf16[128,512]{1,0:T(8,128)(2,1)S(1)}, u32[]{:S(2)}) copy-start(bf16[128,512]{1,0:T(8,128)(2,1)S(1)} %convert_element_type.767) | copy-start | bytes 393220 | tf_op jit(solution)/shard_map/cond
  313.7 9.7 copy-start.93
  326.0 13.2 %copy-start.23 = (f32[128,1024]{1,0:T(8,128)S(1)}, f32[128,1024]{1,0:T(8,128)}, u32[]{:S(2)}) copy-start(f32[128,1024]{1,0:T(8,128)} %get-tuple-element.1132) | copy-start | bytes 1572868 | tf_op jit(solution)/shard_map/cond
  326.0 13.2 %copy-start.142 = (f32[128]{0:T(128)S(1)}, f32[128]{0:T(128)}, u32[]{:S(2)}) copy-start(f32[128]{0:T(128)} %copy-done.141) | copy-start | bytes 1540 | tf_op jit(solution)/shard_map/cond
  327.3 12.0 %copy-start.63 = (f32[127,1024]{1,0:T(8,128)S(1)}, f32[127,1024]{1,0:T(8,128)}, u32[]{:S(2)}) copy-start(f32[127,1024]{1,0:T(8,128)} %slice_add_fusion.27) | copy-start | bytes 1560580 | tf_op jit(solution)/shard_map/cond
  355.1 55.9 %collective-permute-start.9 = (bf16[128,512]{1,0:T(8,128)(2,1)}, bf16[128,512]{1,0:T(8,128)(2,1)S(1)}, u32[]{:S(2)}, u32[]{:S(2)}) collective-permute-start(bf16[128,512]{1,0:T(8,128)(2,1)} %get-tuple-element.1023), channel_id=1, source_target_pairs={{8,0},{16,8},{24,16},{9,1},{17,9},{25,17},{10,2},{18,10},{26,18},{... | collective-permute-start | bytes 393224 | tf_op jit(solution)/shard_map/ppermute | solution.py:16
  412.0 110.8 %copy-start.21 = (bf16[128,512]{1,0:T(8,128)(2,1)S(1)}, bf16[128,512]{1,0:T(8,128)(2,1)}, u32[]{:S(2)}) copy-start(bf16[128,512]{1,0:T(8,128)(2,1)} %get-tuple-element.1493) | copy-start | bytes 393220
  412.8 17.4 %copy-start.143 = (f32[128]{0:T(128)}, f32[128]{0:T(128)S(1)}, u32[]{:S(2)}) copy-start(f32[128]{0:T(128)S(1)} %bitcast_convert_fusion.5) | copy-start | bytes 1540 | tf_op jit(solution)/shard_map/cond
  413.5 13.1 %copy-start.129 = (f32[128]{0:T(128)}, f32[128]{0:T(128)S(1)}, u32[]{:S(2)}) copy-start(f32[128]{0:T(128)S(1)} %fusion.1224) | copy-start | bytes 1540 | tf_op jit(solution)/shard_map/cond
  414.3 12.3 %copy-start.37 = (bf16[128,512]{1,0:T(8,128)(2,1)}, bf16[128,512]{1,0:T(8,128)(2,1)S(1)}, u32[]{:S(2)}) copy-start(bf16[128,512]{1,0:T(8,128)(2,1)S(1)} %fusion.1201) | copy-start | bytes 393220 | tf_op jit(solution)/shard_map/cond
  414.3 12.3 %copy-start.78 = (bf16[128,512]{1,0:T(8,128)(2,1)}, bf16[128,512]{1,0:T(8,128)(2,1)S(1)}, u32[]{:S(2)}) copy-start(bf16[128,512]{1,0:T(8,128)(2,1)S(1)} %convert_element_type.781) | copy-start | bytes 393220 | tf_op jit(solution)/shard_map/cond
  480.3 6.2 copy-start.91
  486.3 13.0 %copy-start.144 = (f32[128]{0:T(128)S(1)}, f32[128]{0:T(128)}, u32[]{:S(2)}) copy-start(f32[128]{0:T(128)} %copy-done.143) | copy-start | bytes 1540 | tf_op jit(solution)/shard_map/cond
  488.2 11.1 %copy-start.64 = (f32[127,1024]{1,0:T(8,128)S(1)}, f32[127,1024]{1,0:T(8,128)}, u32[]{:S(2)}) copy-start(f32[127,1024]{1,0:T(8,128)} %slice_add_fusion.32) | copy-start | bytes 1560580 | tf_op jit(solution)/shard_map/cond
  514.7 8.1 copy-start.18
  514.7 7.1 collective-permute-start.10
  522.8 195.4 %copy-start.15 = (bf16[128,4096]{1,0:T(8,128)(2,1)S(1)}, bf16[128,4096]{1,0:T(8,128)(2,1)}, u32[]{:S(2)}) copy-start(bf16[128,4096]{1,0:T(8,128)(2,1)} %copy-done.14) | copy-start | bytes 3145732
  523.7 20.1 %copy-start.145 = (f32[128]{0:T(128)}, f32[128]{0:T(128)S(1)}, u32[]{:S(2)}) copy-start(f32[128]{0:T(128)S(1)} %bitcast_convert_fusion.6) | copy-start | bytes 1540 | tf_op jit(solution)/shard_map/cond
  609.6 32.8 %copy-start.116 = (f32[1,1024]{1,0:T(1,128)S(1)}, f32[1,1024]{1,0:T(1,128)}, u32[]{:S(2)}) copy-start(f32[1,1024]{1,0:T(1,128)} %slice.5637) | copy-start | bytes 12292 | tf_op jit(solution)/shard_map/cond
  663.1 15.3 %copy-start.105 = (f32[31,1024]{1,0:T(8,128)S(1)}, f32[31,1024]{1,0:T(8,128)}, u32[]{:S(2)}) copy-start(f32[31,1024]{1,0:T(8,128)} %slice.4919) | copy-start | bytes 380932 | tf_op jit(solution)/shard_map/cond
  665.6 22.9 %copy-start.114 = (f32[1,1024]{1,0:T(1,128)S(1)}, f32[1,1024]{1,0:T(1,128)}, u32[]{:S(2)}) copy-start(f32[1,1024]{1,0:T(1,128)} %slice.5611) | copy-start | bytes 12292 | tf_op jit(solution)/shard_map/cond
  678.4 23.0 %copy-start.24 = (f32[128,1024]{1,0:T(8,128)S(1)}, f32[128,1024]{1,0:T(8,128)}, u32[]{:S(2)}) copy-start(f32[128,1024]{1,0:T(8,128)} %get-tuple-element.1140) | copy-start | bytes 1572868 | tf_op jit(solution)/shard_map/cond
  678.4 23.0 %copy-start.146 = (f32[128]{0:T(128)S(1)}, f32[128]{0:T(128)}, u32[]{:S(2)}) copy-start(f32[128]{0:T(128)} %copy-done.145) | copy-start | bytes 1540 | tf_op jit(solution)/shard_map/cond
  717.0 48.7 %collective-permute-start.11 = (bf16[128,512]{1,0:T(8,128)(2,1)}, bf16[128,512]{1,0:T(8,128)(2,1)}, u32[]{:S(2)}, u32[]{:S(2)}) collective-permute-start(bf16[128,512]{1,0:T(8,128)(2,1)} %get-tuple-element.1025), channel_id=1, source_target_pairs={{8,0},{16,8},{24,16},{9,1},{17,9},{25,17},{10,2},{18,10},{26,18},{... | collective-permute-start | bytes 393224 | tf_op jit(solution)/shard_map/ppermute | solution.py:16
  718.3 10.5 copy-start.30
  718.3 10.5 copy-start.71
  728.8 7.7 copy-start.17
  728.8 7.7 copy-start.33
  736.6 6.6 copy-start.36
  736.6 6.6 copy-start.77
  743.1 8.0 copy-start.19
  743.1 8.0 copy-start.39
  757.6 8.0 copy-start.149
  757.6 9.1 copy-start.20
  757.6 9.1 copy-start.42
  757.6 9.1 copy-start.120
  766.8 16.6 %copy-start.147 = (f32[128]{0:T(128)}, f32[128]{0:T(128)S(1)}, u32[]{:S(2)}) copy-start(f32[128]{0:T(128)S(1)} %bitcast_convert_fusion.7) | copy-start | bytes 1540 | tf_op jit(solution)/shard_map/cond
  766.9 12.9 %copy-start.162 = (f32[128]{0:T(128)}, f32[128]{0:T(128)S(1)}, u32[]{:S(2)}) copy-start(f32[128]{0:T(128)S(1)} %fusion.1315) | copy-start | bytes 1540 | tf_op jit(solution)/shard_map/cond
  767.5 9.8 copy-start.40
  767.6 12.2 %copy-start.81 = (bf16[128,512]{1,0:T(8,128)(2,1)}, bf16[128,512]{1,0:T(8,128)(2,1)S(1)}, u32[]{:S(2)}) copy-start(bf16[128,512]{1,0:T(8,128)(2,1)S(1)} %convert_element_type.809) | copy-start | bytes 393220 | tf_op jit(solution)/shard_map/cond
  788.7 17.0 %copy-start.106 = (f32[31,1024]{1,0:T(8,128)S(1)}, f32[31,1024]{1,0:T(8,128)}, u32[]{:S(2)}) copy-start(f32[31,1024]{1,0:T(8,128)} %slice.5089) | copy-start | bytes 380932 | tf_op jit(solution)/shard_map/cond
  825.3 14.5 %copy-start.65 = (f32[127,1024]{1,0:T(8,128)S(1)}, f32[127,1024]{1,0:T(8,128)}, u32[]{:S(2)}) copy-start(f32[127,1024]{1,0:T(8,128)} %slice_add_fusion.42) | copy-start | bytes 1560580 | tf_op jit(solution)/shard_map/cond
  825.3 14.5 %copy-start.148 = (f32[128]{0:T(128)S(1)}, f32[128]{0:T(128)}, u32[]{:S(2)}) copy-start(f32[128]{0:T(128)} %copy-done.147) | copy-start | bytes 1540 | tf_op jit(solution)/shard_map/cond
  928.4 24.3 %collective-permute-start.14 = (bf16[128,512]{1,0:T(8,128)(2,1)S(1)}, bf16[128,512]{1,0:T(8,128)(2,1)S(1)}, u32[]{:S(2)}, u32[]{:S(2)}) collective-permute-start(bf16[128,512]{1,0:T(8,128)(2,1)S(1)} %get-tuple-element.1489), channel_id=1, source_target_pairs={{0,8},{8,16},{16,24},{1,9},{9,17},{17,25},{2,10},{10,18},{18,26},{... | collective-permute-start | bytes 393224 | tf_op jit(solution)/shard_map/ppermute | solution.py:16
  932.6 20.1 %collective-permute-start.13 = (bf16[128,512]{1,0:T(8,128)(2,1)S(1)}, bf16[128,512]{1,0:T(8,128)(2,1)S(1)}, u32[]{:S(2)}, u32[]{:S(2)}) collective-permute-start(bf16[128,512]{1,0:T(8,128)(2,1)S(1)} %get-tuple-element.1490), channel_id=1, source_target_pairs={{0,16},{8,24},{1,17},{9,25},{2,18},{10,26},{3,19},{11,27},{4,20},{... | collective-permute-start | bytes 393224 | tf_op jit(solution)/shard_map/ppermute | solution.py:16
  934.7 18.0 %collective-permute-start.12 = (bf16[128,512]{1,0:T(8,128)(2,1)S(1)}, bf16[128,512]{1,0:T(8,128)(2,1)S(1)}, u32[]{:S(2)}, u32[]{:S(2)}) collective-permute-start(bf16[128,512]{1,0:T(8,128)(2,1)S(1)} %get-tuple-element.1491), channel_id=1, source_target_pairs={{0,24},{1,25},{2,26},{3,27},{4,28},{5,29},{6,30},{7,31}} | collective-permute-start | bytes 393224 | tf_op jit(solution)/shard_map/ppermute | solution.py:16
  (38 other events, 75.6 us)
Sparse Core Ops, SparseCore 0:
  881.0 176.2 all-reduce.317
where the time goes:
time: 1090 us; the launch traced here: 1070 us
  local copies, waits for them, and re-layouts  286 us (26%)
  waiting for transfers between devices  269 us (25%)
  other arithmetic  227 us (21%)
  blocking collectives  102 us (9%)
  loops' own time  69 us (6%)
  matrix products  65.4 us (6%)
  starting transfers between devices  36.5 us (3%)
  between operations  16.6 us (2%)
    slice x492, local copies, waits for them, and re-layouts, recurrence(): return lax.associative_scan(combine, (decay_rate, drive_term), axis=0)[1]  176 us
    ppermute x15, waiting for transfers between devices, from_behind(): return lax.ppermute(shard, axis, pairs)  165 us
    psum x1, waiting for transfers between devices, local(): weight_grads, gain_sums = lax.psum((weight_total, gain_total), 'dp')  104 us
    pad x144, local copies, waits for them, and re-layouts, recurrence(): return lax.associative_scan(combine, (decay_rate, drive_term), axis=0)[1]  61.4 us
    another operation x7, loops' own time, local(): lax.switch(branch_pick, [spare_backward, mixer_back_branch, dense_back_br...  54.4 us
    psum x1, blocking collectives, local(): lax.psum((forget_vector, valid_count), ('section', 'dp'))  41.2 us
    ppermute x15, starting transfers between devices, from_behind(): return lax.ppermute(shard, axis, pairs)  36.5 us
    add x80, other arithmetic, recurrence(): return lax.associative_scan(combine, (decay_rate, drive_term), axis=0)[1]  33.9 us
  transfers between devices with their start and end apart: 16, of which 11 were waited for; matrix products, arithmetic and copies ran while one was open for 5% of the time, Pallas kernels for 0%

commit v1 on v0

v1 whole, which is shorter than its diff:
```python
import functools

import jax
import jax.numpy as jnp
from jax import lax
from jax.experimental import pallas as pl
from jax.experimental.pallas import tpu as pltpu
from jax.sharding import PartitionSpec as P

EPS = 1e-06
MESH = pl.DeviceIdType.MESH
F32 = jnp.float32
BF16 = jnp.bfloat16
LANES = 128
MIX_CHUNK = 256
DENSE_CHUNK = 512
SUM_CHUNK = 128


def dot_nn(left, right):
    return jnp.dot(left, right, preferred_element_type=F32)


def dot_nt(left, right):
    return lax.dot_general(left, right, (((1,), (1,)), ((), ())), preferred_element_type=F32)


def scan_down(decay, drive):
    for by in (1, 2, 4):
        drive = drive + decay * pltpu.roll(drive, by, 0)
        decay = decay * pltpu.roll(decay, by, 0)
    blocks = [drive[:8]]
    for at in range(8, drive.shape[0], 8):
        blocks.append(drive[at : at + 8] + decay[at : at + 8] * blocks[-1])
    return jnp.concatenate(blocks, 0)


def scan_up(decay_next, source):
    rows = source.shape[0]
    for by in (1, 2, 4):
        source = source + decay_next * pltpu.roll(source, rows - by, 0)
        decay_next = decay_next * pltpu.roll(decay_next, rows - by, 0)
    blocks = [source[rows - 8 :]]
    for at in range(rows - 16, -1, -8):
        blocks.append(source[at : at + 8] + decay_next[at : at + 8] * blocks[-1])
    return jnp.concatenate(blocks[::-1], 0)


def wide(column, width):
    return jnp.concatenate([column] * (width // LANES), 1)


def unit(x):
    return lax.rsqrt(jnp.mean(x * x, axis=-1, keepdims=True) + EPS)


def norm_back(x, q, gain, d_normed, grad_out):
    x_hat = x * q
    scaled = d_normed * gain
    mean = jnp.mean(scaled * x_hat, axis=-1, keepdims=True)
    d_gain = jnp.sum(d_normed * x_hat, axis=0, keepdims=True)
    return grad_out + q * (scaled - x_hat * mean), d_gain


def gelu_parts(u):
    cdf = 0.5 * lax.erf(u * 0.7071067811865476) + 0.5
    slope = cdf + u * (0.3989422804014327 * jnp.exp(-0.5 * u * u))
    return u * cdf, slope


def kernel(
    count,
    x_ref, cot_ref, w_hbm, gain_ref, len_ref, fill_ref,
    ig_ref, dw_ref, dgain_ref, fmean_ref,
    w, res, grad, out, gout, dy_own, mask, mask_own,
    decay_next, coef, slope, da, rows, left, forget_acc,
    sib_out, sib_in, outer_in, part, tot_in, work,
    small, small_sib, small_outer, small_part, small_tot, small_far,
    w_sem, x_send, dy_send, mask_send, res_send, res_recv, grad_send, grad_recv, mask_recv, ig_recv,
    sib_send, sib_recv, part_send, outer_recv, tot_send, tot_recv, fin_send, fin_recv,
    small_send, small_recv, far_send, far_recv,
):
    s = lax.axis_index("section")
    d = lax.axis_index("dp")
    core = lax.rem(d, 2)
    chip = d // 2
    chips = count // 2
    sections, slot, width = res.shape
    pack = w.shape[1]
    gate = pack // 4
    ff = pack // 2
    half = pack // 2
    pieces = sib_in.shape[0]
    piece = sib_in.shape[2]
    last = sections - 1
    is_first = s == 0
    is_last = s == last
    is_mixer = lax.rem(s, 2) == 0
    on_left = chip < chips // 2
    is_middle = (chip == chips // 2 - 1) | (chip == chips // 2)
    is_end = (chip == 0) | (chip == chips - 1)
    sibling = (s, d + 1 - 2 * core)
    inner = (s, jnp.where(on_left, d + 2, d - 2))
    outer = (s, jnp.where(on_left, d - 2, d + 2))

    w_copy = pltpu.make_async_copy(w_hbm, w, w_sem)
    w_copy.start()

    barrier = pltpu.get_barrier_semaphore()
    for by in range(1, sections):
        pl.semaphore_signal(barrier, inc=1, device_id=(lax.rem(s + by, sections), d), device_id_type=MESH)
    pl.semaphore_signal(barrier, inc=1, device_id=sibling, device_id_type=MESH)

    @pl.when(chip > 0)
    def _():
        pl.semaphore_signal(barrier, inc=1, device_id=(s, d - 2), device_id_type=MESH)

    @pl.when(chip < chips - 1)
    def _():
        pl.semaphore_signal(barrier, inc=1, device_id=(s, d + 2), device_id_type=MESH)

    def remote(src, dst, send, recv, target):
        return pltpu.make_async_remote_copy(
            src_ref=src, dst_ref=dst, send_sem=send, recv_sem=recv, device_id=target, device_id_type=MESH
        )

    lane = lax.broadcasted_iota(jnp.int32, (8, slot), 1)
    row = lax.broadcasted_iota(jnp.int32, (8, slot), 0)
    starts = lane == 0
    position = len_ref[0, 0, 0]
    for k in range(1, len_ref.shape[2]):
        starts = starts | (lane == position)
        position = position + len_ref[0, 0, k]
    keep_rows = jnp.where(starts, 0.0, 1.0)
    valid_rows = jnp.where(lane < fill_ref[0, 0], 1.0, 0.0)
    mask_own[...] = jnp.where(row == 0, keep_rows, valid_rows)
    tokens = lax.broadcasted_iota(jnp.int32, (slot, width), 0)
    dy_own[...] = jnp.where(tokens < fill_ref[0, 0], cot_ref[0].astype(F32), 0.0).astype(BF16)
    forget_acc[...] = jnp.zeros_like(forget_acc)
    small[...] = jnp.zeros_like(small)

    pl.semaphore_wait(
        barrier, sections + jnp.where(chip > 0, 1, 0) + jnp.where(chip < chips - 1, 1, 0)
    )

    x_copy = remote(x_ref.at[0], res.at[s], x_send, res_recv.at[s], (0, d))
    dy_copy = remote(dy_own, grad.at[s], dy_send, grad_recv.at[s], (last, d))
    mask_copies = [
        remote(mask_own, mask.at[s], mask_send.at[k], mask_recv.at[s], (2 * k, d))
        for k in range(sections // 2)
    ]

    @pl.when(is_first)
    def _():
        res[0] = x_ref[0]

    @pl.when(s != 0)
    def _():
        x_copy.start()

    for k in range(sections // 2):

        @pl.when(s == 2 * k)
        def _():
            mask[s] = mask_own[...]

        @pl.when(s != 2 * k)
        def _():
            mask_copies[k].start()

    @pl.when(is_last)
    def _():
        grad[last] = dy_own[...]

    @pl.when(s != last)
    def _():
        dy_copy.start()

    def res_in(m):
        return remote(out.at[m], res.at[m], res_send.at[m], res_recv.at[m], (jnp.minimum(s + 1, last), d))

    def grad_in(m):
        return remote(gout.at[m], grad.at[m], grad_send.at[m], grad_recv.at[m], (jnp.maximum(s - 1, 0), d))

    def wait_res(m):
        @pl.when((s != 0) | (m != 0))
        def _():
            res_in(m).wait_recv()

    def wait_grad(m):
        @pl.when((s != last) | (m != last))
        def _():
            grad_in(m).wait_recv()

    def send_grad(m):
        @pl.when(s != 0)
        def _():
            grad_in(m).start()

        @pl.when((s == 0) & (m == 0))
        def _():
            ig_ref[0] = gout[m]

        @pl.when((s == 0) & (m != 0))
        def _():
            remote(gout.at[m], ig_ref.at[0], grad_send.at[m], ig_recv, (m, d)).start()

    gain = gain_ref[...]
    w_copy.wait()

    @pl.when(is_mixer)
    def _():
        def forward(m, carry):
            wait_res(m)

            @pl.when(m != s)
            def _():
                remote(mask_own, mask.at[m], mask_send.at[0], mask_recv.at[m], (0, d)).wait_recv()

            at = pl.ds(pl.multiple_of(m * slot, slot), slot)
            masks = mask[m]
            keep = wide(jnp.broadcast_to(masks[0:1], (slot, slot)).T, MIX_CHUNK)
            valid = wide(jnp.broadcast_to(masks[1:2], (slot, slot)).T, MIX_CHUNK)
            x = res[m].astype(F32)
            normed = (x * unit(x) * gain).astype(BF16)
            total = x
            for c in range(0, gate, MIX_CHUNK):
                f_in = dot_nn(normed, w[:, c : c + MIX_CHUNK])
                i_in = dot_nn(normed, w[:, gate + c : gate + c + MIX_CHUNK])
                c_in = dot_nn(normed, w[:, 2 * gate + c : 2 * gate + c + MIX_CHUNK])
                top = jnp.maximum(jnp.maximum(-f_in, -i_in), 0.0)
                e_zero = jnp.exp(-top)
                e_f = jnp.exp(-f_in - top)
                e_i = jnp.exp(-i_in - top)
                u_f = e_zero + e_f
                u_i = e_zero + e_i
                inv = 1.0 / (u_f + u_i)
                forget = u_i * inv
                intake = u_f * inv
                e_c = jnp.exp(-jnp.abs(c_in))
                soft = jnp.maximum(c_in, 0.0) + jnp.log1p(e_c)
                decay = forget * keep
                state = scan_down(decay, intake * soft)
                state_low = state.astype(BF16)
                total = total + dot_nt(state_low, w[:, 3 * gate + c : 3 * gate + c + MIX_CHUNK])
                rows[at, 3 * gate + c : 3 * gate + c + MIX_CHUNK] = state_low
                bend = soft - keep * pltpu.roll(state, 1, 0)
                decay_next[m, :, c : c + MIX_CHUNK] = pltpu.roll(decay, slot - 1, 0)
                coef[m, :, c : c + MIX_CHUNK] = -forget * (e_f * inv) * bend
                coef[m, :, gate + c : gate + c + MIX_CHUNK] = intake * (e_i * inv) * bend
                coef[m, :, 2 * gate + c : 2 * gate + c + MIX_CHUNK] = (
                    intake * jnp.where(c_in >= 0.0, 1.0, e_c) / (1.0 + e_c)
                )
                counted = forget * valid
                folded = counted[:8]
                for k in range(8, slot, 8):
                    folded = folded + counted[k : k + 8]
                forget_acc[...] += folded
            out[m] = total.astype(BF16)
            res_in(m).start()
            left[0, :, at] = normed.astype(F32).T.astype(BF16)
            return carry

        lax.fori_loop(0, sections, forward, 0)

        def backward(m, carry):
            wait_grad(m)
            at = pl.ds(pl.multiple_of(m * slot, slot), slot)
            g_low = grad[m]
            x = res[m].astype(F32)
            q = unit(x)
            d_normed = jnp.zeros((slot, width), F32)
            for c in range(0, gate, MIX_CHUNK):
                d_state = dot_nn(g_low, w[:, 3 * gate + c : 3 * gate + c + MIX_CHUNK])
                adjoint = scan_up(decay_next[m, :, c : c + MIX_CHUNK], d_state)
                for k in range(3):
                    part_at = slice(k * gate + c, k * gate + c + MIX_CHUNK)
                    low = (adjoint * coef[m, :, part_at]).astype(BF16)
                    rows[at, part_at] = low
                    d_normed = d_normed + dot_nt(low, w[:, part_at])
            g_high = g_low.astype(F32)
            d_res, d_gain = norm_back(x, q, gain, d_normed, g_high)
            gout[m] = d_res.astype(BF16)
            send_grad(m)
            small[0:1, :] += d_gain
            left[1, :, at] = g_high.T.astype(BF16)
            return carry

        lax.fori_loop(0, sections, backward, 0)

    @pl.when((lax.rem(s, 2) == 1) & (s != last))
    def _():
        def forward(m, carry):
            wait_res(m)
            at = pl.ds(pl.multiple_of(m * slot, slot), slot)
            x = res[m].astype(F32)
            normed = (x * unit(x) * gain).astype(BF16)
            total = x
            for c in range(0, ff, DENSE_CHUNK):
                hidden, bend = gelu_parts(dot_nn(normed, w[:, c : c + DENSE_CHUNK]))
                low = hidden.astype(BF16)
                total = total + dot_nt(low, w[:, ff + c : ff + c + DENSE_CHUNK])
                rows[at, ff + c : ff + c + DENSE_CHUNK] = low
                slope[m, :, c : c + DENSE_CHUNK] = bend
            out[m] = total.astype(BF16)
            res_in(m).start()
            left[0, :, at] = normed.astype(F32).T.astype(BF16)
            return carry

        lax.fori_loop(0, sections, forward, 0)

        def backward(m, carry):
            wait_grad(m)
            at = pl.ds(pl.multiple_of(m * slot, slot), slot)
            g_low = grad[m]
            x = res[m].astype(F32)
            q = unit(x)
            d_normed = jnp.zeros((slot, width), F32)
            for c in range(0, ff, DENSE_CHUNK):
                d_act = dot_nn(g_low, w[:, ff + c : ff + c + DENSE_CHUNK])
                low = (d_act * slope[m, :, c : c + DENSE_CHUNK]).astype(BF16)
                rows[at, c : c + DENSE_CHUNK] = low
                d_normed = d_normed + dot_nt(low, w[:, c : c + DENSE_CHUNK])
            g_high = g_low.astype(F32)
            d_res, d_gain = norm_back(x, q, gain, d_normed, g_high)
            gout[m] = d_res.astype(BF16)
            send_grad(m)
            small[0:1, :] += d_gain
            left[1, :, at] = g_high.T.astype(BF16)
            return carry

        lax.fori_loop(0, sections, backward, 0)

    @pl.when(is_last)
    def _():
        def prepare(m, carry):
            wait_grad(m)
            at = pl.ds(pl.multiple_of(m * slot, slot), slot)
            g_low = grad[m]
            for c in range(0, ff, DENSE_CHUNK):
                da[m, :, c : c + DENSE_CHUNK] = dot_nn(g_low, w[:, ff + c : ff + c + DENSE_CHUNK])
            left[1, :, at] = g_low.astype(F32).T.astype(BF16)
            return carry

        lax.fori_loop(0, sections, prepare, 0)

        def both(m, carry):
            wait_res(m)
            at = pl.ds(pl.multiple_of(m * slot, slot), slot)
            x = res[m].astype(F32)
            q = unit(x)
            normed = (x * q * gain).astype(BF16)
            d_normed = jnp.zeros((slot, width), F32)
            for c in range(0, ff, DENSE_CHUNK):
                hidden, bend = gelu_parts(dot_nn(normed, w[:, c : c + DENSE_CHUNK]))
                rows[at, ff + c : ff + c + DENSE_CHUNK] = hidden.astype(BF16)
                low = (da[m, :, c : c + DENSE_CHUNK] * bend).astype(BF16)
                rows[at, c : c + DENSE_CHUNK] = low
                d_normed = d_normed + dot_nt(low, w[:, c : c + DENSE_CHUNK])
            d_res, d_gain = norm_back(x, q, gain, d_normed, grad[m].astype(F32))
            gout[m] = d_res.astype(BF16)
            send_grad(m)
            small[0:1, :] += d_gain
            left[0, :, at] = normed.astype(F32).T.astype(BF16)
            return carry

        lax.fori_loop(0, sections, both, 0)

    @pl.when(is_mixer)
    def _():
        small[1:2, 0:MIX_CHUNK] = jnp.sum(forget_acc[...], axis=0, keepdims=True)
        used = mask[0, 1:2]
        for m in range(1, sections):
            used = used + mask[m, 1:2]
        small[2:3, 0:slot] = used

    split = jnp.where(is_mixer, 3 * gate, ff)

    def grad_piece(col):
        side = jnp.where(col < split, 0, 1)
        return dot_nn(left[side], rows[:, pl.ds(pl.multiple_of(col, piece), piece)])

    def sib_copy(k):
        return remote(sib_out.at[k], sib_in.at[k], sib_send.at[k], sib_recv.at[k], sibling)

    def inward(k):
        return remote(part.at[k], outer_in.at[k], part_send.at[k], outer_recv.at[k], inner)

    def across(k):
        return remote(part.at[k], tot_in.at[k], part_send.at[k], tot_recv.at[k], inner)

    def outward(k):
        return remote(tot_in.at[k], tot_in.at[k], tot_send.at[k], tot_recv.at[k], outer)

    def own_at(k):
        return pl.ds(pl.multiple_of(core * half + k * piece, piece), piece)

    def final(k):
        return remote(tot_in.at[k], dw_ref.at[:, own_at(k)], fin_send.at[k], fin_recv.at[k], sibling)

    small_swap = remote(small, small_sib, small_send.at[0], small_recv.at[0], sibling)
    small_inward = remote(small_part, small_outer, small_send.at[1], small_recv.at[1], inner)
    small_across = remote(small_part, small_tot, small_send.at[1], small_recv.at[2], inner)
    small_outward = remote(small_tot, small_tot, small_send.at[2], small_recv.at[2], outer)

    small_swap.start()

    def to_sibling(k, carry):
        sib_out[k] = grad_piece((1 - core) * half + k * piece).astype(BF16)
        sib_copy(k).start()
        return carry

    lax.fori_loop(0, pieces, to_sibling, 0)

    def reduce_small():
        small_swap.wait_recv()

        @pl.when(is_end)
        def _():
            small_part[...] = small[...] + small_sib[...]

        @pl.when(jnp.logical_not(is_end))
        def _():
            small_inward.wait_recv()
            small_part[...] = small[...] + small_sib[...] + small_outer[...]

        @pl.when(is_middle)
        def _():
            small_across.start()

        @pl.when(jnp.logical_not(is_middle))
        def _():
            small_inward.start()

    def far_copy(k):
        return remote(
            small_tot, small_far.at[s // 2], far_send.at[k - 1], far_recv.at[s // 2], (lax.rem(s + k, sections), d)
        )

    def total_small():
        small_across.wait_recv()

        @pl.when(is_middle)
        def _():
            small_tot[...] = small_tot[...] + small_part[...]

        @pl.when(jnp.logical_not(is_end))
        def _():
            small_outward.start()

        @pl.when(is_mixer)
        def _():
            small_far[s // 2] = small_tot[...]
            for k in range(1, sections):
                far_copy(k).start()

    def reduce_piece(k):
        work[...] = grad_piece(core * half + k * piece)
        sib_copy(k).wait_recv()

        @pl.when(is_end)
        def _():
            part[k] = (work[...] + sib_in[k].astype(F32)).astype(BF16)

        @pl.when(jnp.logical_not(is_end))
        def _():
            inward(k).wait_recv()
            part[k] = (work[...] + sib_in[k].astype(F32) + outer_in[k].astype(F32)).astype(BF16)

        @pl.when(is_middle)
        def _():
            across(k).start()

        @pl.when(jnp.logical_not(is_middle))
        def _():
            inward(k).start()

    def total_piece(k):
        across(k).wait_recv()

        @pl.when(is_middle)
        def _():
            tot_in[k] = (tot_in[k].astype(F32) + part[k].astype(F32)).astype(BF16)

        @pl.when(jnp.logical_not(is_end))
        def _():
            outward(k).start()

        final(k).start()
        dw_ref[:, own_at(k)] = tot_in[k]

    lag = jnp.where(is_middle, 2, pieces)

    def step(i, carry):
        @pl.when(i == 0)
        def _():
            reduce_small()

        @pl.when(i < pieces)
        def _():
            reduce_piece(i)

        @pl.when(i == lag)
        def _():
            total_small()

        @pl.when(i >= lag)
        def _():
            total_piece(i - lag)

        return carry

    lax.fori_loop(0, pieces + lag, step, 0)

    for k in range(sections // 2):

        @pl.when(s != 2 * k)
        def _():
            remote(small_tot, small_far.at[k], far_send.at[0], far_recv.at[k], sibling).wait_recv()

    dgain_ref[...] = small_tot[0:1, :]
    lanes = lax.broadcasted_iota(jnp.int32, (1, LANES), 1)
    means = jnp.zeros((1, LANES), F32)
    for k in range(sections // 2):
        sums = jnp.sum(small_far[k], axis=1, keepdims=True)
        means = jnp.where(lanes == k, sums[1:2] / (sums[2:3] * gate), means)
    fmean_ref[...] = means

    @pl.when(s != 0)
    def _():
        remote(gout.at[0], ig_ref.at[0], grad_send.at[0], ig_recv, (s, d)).wait_recv()
        x_copy.wait_send()

    @pl.when(s != last)
    def _():
        dy_copy.wait_send()

    for k in range(sections // 2):

        @pl.when(s != 2 * k)
        def _():
            mask_copies[k].wait_send()

    for m in range(sections):

        @pl.when(s != last)
        def _():
            res_in(m).wait_send()

        @pl.when((s != 0) | (m != 0))
        def _():
            grad_in(m).wait_send()

    small_swap.wait_send()
    small_across.wait_send()

    @pl.when(jnp.logical_not(is_end))
    def _():
        small_outward.wait_send()

    @pl.when(is_mixer)
    def _():
        for k in range(1, sections):
            far_copy(k).wait_send()

    def finish(k, carry):
        sib_copy(k).wait_send()
        across(k).wait_send()

        @pl.when(jnp.logical_not(is_end))
        def _():
            outward(k).wait_send()

        final(k).wait()
        return carry

    lax.fori_loop(0, pieces, finish, 0)


def local(count, inputs, cotangent, section_weights, norm_gains, doc_lengths, slot_fill):
    sections = lax.axis_size("section")
    slot, width = inputs.shape[1:]
    pack = section_weights.shape[1]
    gate, ff, half = pack // 4, pack // 2, pack // 2
    tokens = sections * slot
    pieces = half // SUM_CHUNK
    dma = pltpu.SemaphoreType.DMA
    halves = pltpu.VMEM((pieces, width, SUM_CHUNK), BF16)
    small = pltpu.VMEM((8, width), F32)
    stack = pltpu.VMEM((sections, slot, width), BF16)
    vmem = pl.BlockSpec(memory_space=pltpu.VMEM)
    smem = pl.BlockSpec(memory_space=pltpu.SMEM)
    input_grad, weight_grads, gain_grads, means = pl.pallas_call(
        functools.partial(kernel, count),
        out_shape=(
            jax.ShapeDtypeStruct((1, slot, width), BF16),
            jax.ShapeDtypeStruct((width, pack), BF16),
            jax.ShapeDtypeStruct((1, width), F32),
            jax.ShapeDtypeStruct((1, LANES), F32),
        ),
        in_specs=[vmem, vmem, pl.BlockSpec(memory_space=pl.ANY), vmem, smem, smem],
        out_specs=(vmem, vmem, vmem, vmem),
        scratch_shapes=[
            pltpu.VMEM((width, pack), BF16),
            stack, stack, stack, stack,
            pltpu.VMEM((slot, width), BF16),
            pltpu.VMEM((sections, 8, slot), F32),
            pltpu.VMEM((8, slot), F32),
            pltpu.VMEM((sections, slot, gate), F32),
            pltpu.VMEM((sections, slot, 3 * gate), F32),
            pltpu.VMEM((sections, slot, ff), F32),
            pltpu.VMEM((sections, slot, ff), F32),
            pltpu.VMEM((tokens, pack), BF16),
            pltpu.VMEM((2, width, tokens), BF16),
            pltpu.VMEM((8, MIX_CHUNK), F32),
            halves, halves, halves, halves, halves,
            pltpu.VMEM((width, SUM_CHUNK), F32),
            small, small, small, small, small,
            pltpu.VMEM((sections // 2, 8, width), F32),
            dma, dma, dma,
            dma((sections // 2,)),
            dma((sections,)), dma((sections,)), dma((sections,)), dma((sections,)),
            dma((sections,)), dma,
            dma((pieces,)), dma((pieces,)), dma((pieces,)), dma((pieces,)),
            dma((pieces,)), dma((pieces,)), dma((pieces,)), dma((pieces,)),
            dma((3,)), dma((3,)), dma((sections - 1,)), dma((sections // 2,)),
        ],
        compiler_params=pltpu.CompilerParams(
            collective_id=0, has_side_effects=True, vmem_limit_bytes=56 * 1024 * 1024
        ),
    )(inputs, cotangent, section_weights, norm_gains.reshape(1, width), doc_lengths, slot_fill)
    return (
        input_grad,
        weight_grads.astype(F32),
        gain_grads.reshape(width),
        means[0, : sections // 2],
    )


def solution(mesh):
    placed = (
        P("section", "dp", None),
        P("section", "dp", None),
        P("section", None),
        P("section"),
        P("section", "dp", None),
        P("section", "dp"),
    )
    return jax.shard_map(
        functools.partial(local, mesh.shape["dp"]),
        mesh=mesh,
        in_specs=placed,
        out_specs=(P("section", "dp", None), P("section", None), P("section"), P()),
        check_vma=False,
    )
```

time: 1090 us -> 133 us (0.12); the launches traced: 1070 us -> 132 us
  local copies, waits for them, and re-layouts: 286 us -> 2.36 us
  waiting for transfers between devices: 269 us -> 0 us
  other arithmetic: 227 us -> 6.7 us
  Pallas kernels: 0 us -> 122 us
  blocking collectives: 102 us -> 0 us
  loops' own time: 69 us -> 0 us
  matrix products: 65.4 us -> 0 us
  starting transfers between devices: 36.5 us -> 0 us
  between operations: 16.6 us -> 1.29 us
    slice x496 -> x0, local copies, waits for them, and re-layouts: 177 us -> none  [the longest x492 176 us: recurrence(): return lax.associative_scan(combine, (decay_rate, drive_term), axis=0)[1]]
    ppermute x15 -> x0, waiting for transfers between devices: 165 us -> none  [from_behind(): return lax.ppermute(shard, axis, pairs)]
    pallas_call x0 -> x1, Pallas kernels: none -> 122 us  [local(): pl.pallas_call(functools.partial(kernel, count), out_shape=(jax.ShapeDtyp...]
    psum x1 -> x0, waiting for transfers between devices: 104 us -> none  [local(): weight_grads, gain_sums = lax.psum((weight_total, gain_total), 'dp')]
    add x162 -> x0, other arithmetic: 79.8 us -> none  [the longest x80 33.9 us: recurrence(): return lax.associative_scan(combine, (decay_rate, drive_term), axis=0)[1]]
    another operation x21 -> x0, loops' own time: 69 us -> none  [the longest x7 54.4 us: local(): lax.switch(branch_pick, [spare_backward, mixer_back_branch, dense_back_br...]
    dot_general x34 -> x0, matrix products: 65.4 us -> none  [the longest x14 24.9 us: contract_rows(): lax.dot_general(left, right, (((0,), (0,)), ((), ())), preferred_element_...]
    pad x144 -> x0, local copies, waits for them, and re-layouts: 61.4 us -> none  [recurrence(): return lax.associative_scan(combine, (decay_rate, drive_term), axis=0)[1]]
  transfers between devices with their start and end apart: 16 -> 0, of which waited for: 11 -> 0; matrix products, arithmetic and copies ran while one was open for 5% -> 0% of each run, Pallas kernels for 0% -> 0%
where the time goes in v1:
time: 133 us; the launch traced here: 132 us
  Pallas kernels  122 us (92%)
  other arithmetic  6.7 us (5%)
  local copies, waits for them, and re-layouts  2.36 us (2%)
    pallas_call x1, Pallas kernels, local(): pl.pallas_call(functools.partial(kernel, count), out_shape=(jax.ShapeDtyp...  122 us
    convert_element_type x1, other arithmetic, local(): weight_grads.astype(F32)  6.7 us

profile of v1, /device:TPU:0, one launch (start us, length us, event | category | flops | bytes accessed | tf_op | source)
XLA Modules:
  0.0 132.4 jit_solution(3148831181073320075)
XLA Ops:
  1.3 122.0 %shard_map.93 = (bf16[1,128,512]{2,1,0:T(8,128)(2,1)}, bf16[512,4096]{1,0:T(8,128)(2,1)}, f32[1,512]{1,0:T(1,128)}, f32[1,128]{1,0:T(1,128)}) custom-call(bf16[1,128,512]{2,1,0:T(8,128)(2,1)} %x_ref.1, bf16[1,128,512]{2,1,0:T(8,128)(2,1)} %cot_ref.1, bf16[512,4096]{1,0:T(8,128)(2,1)} %w_hbm.1, f32[1,512]{1,0:T(1,128)} %bitcast.4, s32[1,1,6]{2,1,0:T(1,128)} %len_ref.1, ...), custom_call_target="tpu_custom_call" | custom-call | tf_op jit(solution)/shard_map/pallas_call | solution.py:593
  123.3 1.1 slice_bitcast_fusion
  124.4 0.0 copy-start
  124.4 0.0 copy-start.1
  124.4 6.7 %convert_element_type.3 = f32[512,4096]{1,0:T(8,128)} convert(bf16[512,4096]{1,0:T(8,128)(2,1)} %get-tuple-element.9) | non-fusion elementwise | flops 2097152 | bytes 12582912 | tf_op jit(solution)/shard_map/convert_element_type | solution.py:634
  131.1 0.0 copy-done
  131.1 0.7 copy.13
  131.8 0.0 copy-done.1
  131.8 0.6 copy.14
Async XLA Ops:
  124.4 6.7 %copy-start = (bf16[1,128,512]{2,1,0:T(8,128)(2,1)S(1)}, bf16[1,128,512]{2,1,0:T(8,128)(2,1)}, u32[]{:S(2)}) copy-start(bf16[1,128,512]{2,1,0:T(8,128)(2,1)} %get-tuple-element.16) | copy-start | bytes 393220
  124.4 7.4 %copy-start.1 = (f32[1,512]{1,0:T(1,128)S(1)}, f32[1,512]{1,0:T(1,128)}, u32[]{:S(2)}) copy-start(f32[1,512]{1,0:T(1,128)} %get-tuple-element.10) | copy-start | bytes 6148

commit v2 on v1

v2 whole, which is shorter than its diff:
```python
import functools

import jax
import jax.numpy as jnp
from jax import lax
from jax.experimental import pallas as pl
from jax.experimental.pallas import tpu as pltpu
from jax.sharding import PartitionSpec as P

EPS = 1e-06
MESH = pl.DeviceIdType.MESH
F32 = jnp.float32
BF16 = jnp.bfloat16
LANES = 128
GATE_CHUNK = 256
BACK_CHUNK = 512
DENSE_CHUNK = 512
LAST_CHUNK = 256
TURN = 256
PIECE = (256, 128)
GUESTS = 5
LAG = 3
SMALL_STEP = 3
FINISH_ROWS = 32


def dot(left, right):
    return jnp.dot(left, right, preferred_element_type=F32)


def time_of_row(slot, shape, axis):
    row = lax.broadcasted_iota(jnp.int32, shape, axis)
    return (row & 7) * (slot // 8) + (row >> 3)


def scan_down(decay, drive):
    blocks = range(8, decay.shape[0], 8)
    factor, value = [decay[:8]], [drive[:8]]
    for at in blocks:
        here = decay[at : at + 8]
        value.append(drive[at : at + 8] + here * value[-1])
        factor.append(here * factor[-1])
    joined, through = value[-1], factor[-1]
    for by in (1, 2, 4):
        joined = joined + through * pltpu.roll(joined, by, 0)
        through = through * pltpu.roll(through, by, 0)
    before = pltpu.roll(joined, 1, 0)
    state = [v + f * before for v, f in zip(value, factor)]
    return jnp.concatenate(state, 0), jnp.concatenate([before] + state[:-1], 0)


def scan_up(decay, source):
    rows = decay.shape[0]
    ahead = [decay[at : at + 8] for at in range(8, rows, 8)] + [pltpu.roll(decay[:8], 7, 0)]
    factor, value = [ahead[-1]], [source[rows - 8 :]]
    for k in range(rows // 8 - 2, -1, -1):
        value.append(source[8 * k : 8 * k + 8] + ahead[k] * value[-1])
        factor.append(ahead[k] * factor[-1])
    joined, through = value[-1], factor[-1]
    for by in (1, 2, 4):
        joined = joined + through * pltpu.roll(joined, 8 - by, 0)
        through = through * pltpu.roll(through, 8 - by, 0)
    after = pltpu.roll(joined, 7, 0)
    return jnp.concatenate([v + f * after for v, f in zip(value[::-1], factor[::-1])], 0)


def ahead_of(starts, compute):
    coming = compute(starts[0])
    for k, start in enumerate(starts):
        now = coming
        if k + 1 < len(starts):
            coming = compute(starts[k + 1])
        yield start, now


def wide(column, width):
    return jnp.concatenate([column] * (width // LANES), 1)


def unit(x):
    return lax.rsqrt(jnp.mean(x * x, axis=-1, keepdims=True) + EPS)


def norm_back(x, q, gain, d_normed, grad_out):
    x_hat = x * q
    scaled = d_normed * gain
    mean = jnp.mean(scaled * x_hat, axis=-1, keepdims=True)
    d_gain = jnp.sum(d_normed * x_hat, axis=0, keepdims=True)
    return grad_out + q * (scaled - x_hat * mean), d_gain


def gelu_parts(u):
    cdf = 0.5 * lax.erf(u * 0.7071067811865476) + 0.5
    slope = cdf + u * (0.3989422804014327 * jnp.exp(-0.5 * u * u))
    return u * cdf, slope


def kernel(
    count,
    x_hbm, cot_hbm, w_hbm, gain_hbm, len_hbm, fill_hbm,
    ig_ref, dw_ref, dgain_ref, fmean_ref,
    w, wt, res, grad, out, gout, normal, x_own, dy_own, mask, mask_own, keep_col, valid_col, x_ref, cot_ref, gain_ref, len_ref, fill_ref,
    stash, rows, left, forget_acc,
    sib_out, sib_in, outer_in, part, tot_in, guest_in, work,
    small, small_sib, small_outer, small_part, small_tot, small_far,
    w_sem, load_sem, x_send, dy_send, mask_send, res_send, res_recv, grad_send, grad_recv, mask_recv, ig_recv,
    sib_send, sib_recv, part_send, outer_recv, tot_send, tot_recv, fin_send, fin_recv, guest_recv, back_send,
    small_send, small_recv, far_send, far_recv,
):
    s = lax.axis_index("section")
    d = lax.axis_index("dp")
    core = lax.rem(d, 2)
    chip = d // 2
    chips = count // 2
    sections, slot = mask.shape[0], mask.shape[2]
    tokens, width = res.shape
    pack = w.shape[1]
    gate = pack // 4
    ff = pack // 2
    half = pack // 2
    pieces = sib_in.shape[0]
    guests = guest_in.shape[0]
    piece_rows, piece = sib_in.shape[1:]
    stacked = width // piece_rows
    last = sections - 1
    giver, host = 0, last
    is_first = s == 0
    is_last = s == last
    is_mixer = lax.rem(s, 2) == 0
    on_left = chip < chips // 2
    is_middle = (chip == chips // 2 - 1) | (chip == chips // 2)
    is_end = (chip == 0) | (chip == chips - 1)
    other = d + 1 - 2 * core
    sibling = (s, other)
    inner = (s, jnp.where(on_left, d + 2, d - 2))
    outer = (s, jnp.where(on_left, d - 2, d + 2))

    loads = [
        pltpu.make_async_copy(src, dst, load_sem.at[k])
        for k, (src, dst) in enumerate(
            ((x_hbm, x_ref), (len_hbm, len_ref), (fill_hbm, fill_ref), (cot_hbm, cot_ref), (gain_hbm, gain_ref))
        )
    ]
    w_copy = pltpu.make_async_copy(w_hbm, w, w_sem)
    for load in loads:
        load.start()
    w_copy.start()

    barrier = pltpu.get_barrier_semaphore()
    for by in range(1, sections):
        for lane_of in (d, other):
            pl.semaphore_signal(
                barrier, inc=1, device_id=(lax.rem(s + by, sections), lane_of), device_id_type=MESH
            )
    pl.semaphore_signal(barrier, inc=1, device_id=sibling, device_id_type=MESH)

    @pl.when(chip > 0)
    def _():
        pl.semaphore_signal(barrier, inc=1, device_id=(s, d - 2), device_id_type=MESH)

    @pl.when(chip < chips - 1)
    def _():
        pl.semaphore_signal(barrier, inc=1, device_id=(s, d + 2), device_id_type=MESH)

    def remote(src, dst, send, recv, target):
        return pltpu.make_async_remote_copy(
            src_ref=src, dst_ref=dst, send_sem=send, recv_sem=recv, device_id=target, device_id_type=MESH
        )

    order = jnp.where(
        lax.broadcasted_iota(jnp.int32, (slot, slot), 1) == time_of_row(slot, (slot, slot), 0), 1.0, 0.0
    )
    order_low = order.astype(BF16)
    for load in loads:
        load.wait()
    x_own[...] = dot(order_low, x_ref[0]).astype(BF16)
    lane = lax.broadcasted_iota(jnp.int32, (8, slot), 1)
    row = lax.broadcasted_iota(jnp.int32, (8, slot), 0)
    starts = lane == 0
    position = len_ref[0, 0, 0]
    for k in range(1, len_ref.shape[2]):
        starts = starts | (lane == position)
        position = position + len_ref[0, 0, k]
    keep_rows = jnp.where(starts, 0.0, 1.0)
    valid_rows = jnp.where(lane < fill_ref[0, 0], 1.0, 0.0)
    mask_own[...] = jnp.where(row == 0, keep_rows, valid_rows)
    used_rows = jnp.where(time_of_row(slot, (slot, LANES), 0) < fill_ref[0, 0], 1.0, 0.0)
    dy_own[...] = (dot(order_low, cot_ref[0]) * wide(used_rows, width)).astype(BF16)
    forget_acc[...] = jnp.zeros_like(forget_acc)
    small[...] = jnp.zeros_like(small)

    def whole(m):
        return pl.ds(pl.multiple_of(m * slot, slot), slot)

    def res_in(m):
        return remote(
            out.at[whole(m)], res.at[whole(m)], res_send.at[m], res_recv.at[m], (jnp.minimum(s + 1, last), other)
        )

    def grad_in(m):
        return remote(
            gout.at[whole(m)], grad.at[whole(m)], grad_send.at[m], grad_recv.at[m], (jnp.maximum(s - 1, 0), other)
        )

    def home(m, to):
        return remote(gout.at[whole(m)], ig_ref.at[0], grad_send.at[m], ig_recv, (to, d))

    def wait_res(m):
        @pl.when((s != 0) | (m != 0))
        def _():
            res_in(m).wait_recv()

    def send_grad(m):
        @pl.when((s != 0) & (m > 0))
        def _():
            grad_in(m - 1).wait_send()

        @pl.when(s != 0)
        def _():
            grad_in(m).start()

        @pl.when((s == 0) & (m == 0))
        def _():
            ig_ref[0] = gout[whole(m)]

        @pl.when((s == 0) & (m != 0))
        def _():
            home(m, m).start()

    def turn(side, source, m):
        at = whole(m)
        left[side, :, at] = source[at].T

    def turn_weights(start, stop):
        def one(k, carry):
            at = pl.ds(pl.multiple_of(k * TURN, TURN), TURN)
            wt[at, :] = w[:, at].T
            return carry

        lax.fori_loop(start, stop, one, 0)

    def norm_in(m):
        x = res[whole(m)].astype(F32)
        q = unit(x)
        return x, q, (x * q * gain).astype(BF16)

    def finish_back(m, x, q, d_normed):
        d_res, d_gain = norm_back(x, q, gain, d_normed, grad[whole(m)].astype(F32))
        gout[whole(m)] = d_res.astype(BF16)
        send_grad(m)
        small[0:1, :] += d_gain

    gain = gain_ref[...]

    def mixer_forward(m):
        at = whole(m)
        masks = mask[m]
        keep_col[...] = jnp.broadcast_to(jnp.sum(order * masks[0:1], axis=1, keepdims=True), (slot, LANES))
        valid_col[...] = jnp.broadcast_to(jnp.sum(order * masks[1:2], axis=1, keepdims=True), (slot, LANES))
        wait_res(m)
        keep = wide(keep_col[...], GATE_CHUNK)
        valid = wide(valid_col[...], GATE_CHUNK)
        x, _, normed = norm_in(m)
        normal[at] = normed
        total = x

        def project(c):
            return [dot(normed, w[:, k * gate + c : k * gate + c + GATE_CHUNK]) for k in range(3)]

        for c, (f_in, i_in, c_in) in ahead_of(range(0, gate, GATE_CHUNK), project):
            top = jnp.maximum(jnp.maximum(-f_in, -i_in), 0.0)
            e_zero = jnp.exp(-top)
            e_f = jnp.exp(-f_in - top)
            e_i = jnp.exp(-i_in - top)
            u_f = e_zero + e_f
            u_i = e_zero + e_i
            inv = 1.0 / (u_f + u_i)
            forget = u_i * inv
            intake = u_f * inv
            e_c = jnp.exp(-jnp.abs(c_in))
            soft = jnp.maximum(c_in, 0.0) + jnp.log1p(e_c)
            decay = forget * keep
            state, previous = scan_down(decay, intake * soft)
            state_low = state.astype(BF16)
            total = total + dot(state_low, wt[3 * gate + c : 3 * gate + c + GATE_CHUNK, :])
            rows[at, 3 * gate + c : 3 * gate + c + GATE_CHUNK] = state_low
            bend = soft - keep * previous
            stash[at, c : c + GATE_CHUNK] = -forget * (e_f * inv) * bend
            stash[at, gate + c : gate + c + GATE_CHUNK] = intake * (e_i * inv) * bend
            stash[at, 2 * gate + c : 2 * gate + c + GATE_CHUNK] = (
                intake * jnp.where(c_in >= 0.0, 1.0, e_c) / (1.0 + e_c)
            )
            stash[at, 3 * gate + c : 3 * gate + c + GATE_CHUNK] = decay
            counted = forget * valid
            folded = counted[:8]
            for k in range(8, slot, 8):
                folded = folded + counted[k : k + 8]
            forget_acc[...] += folded
        out[at] = total.astype(BF16)

    inner_turns = 3 * gate // TURN

    @pl.when(is_first)
    def _():
        res[0:slot] = x_own[...]
        mask[0] = mask_own[...]
        w_copy.wait()
        turn_weights(inner_turns, pack // TURN)
        mixer_forward(0)

    pl.semaphore_wait(
        barrier, 2 * sections - 1 + jnp.where(chip > 0, 1, 0) + jnp.where(chip < chips - 1, 1, 0)
    )

    x_copy = remote(x_own, res.at[whole(s)], x_send, res_recv.at[s], (0, d))
    dy_copy = remote(
        dy_own, grad.at[whole(s)], dy_send, grad_recv.at[s], (last, jnp.where(last % 2 == 1, other, d))
    )
    mask_copies = [
        remote(mask_own, mask.at[s], mask_send.at[k], mask_recv.at[s], (2 * k, d))
        for k in range(sections // 2)
    ]

    for k in range(sections // 2):

        @pl.when((s == 2 * k) & (s != 0))
        def _():
            mask[s] = mask_own[...]

        @pl.when(s != 2 * k)
        def _():
            mask_copies[k].start()

    def start_first():
        @pl.when(is_first)
        def _():
            res_in(0).start()

        @pl.when(s != 0)
        def _():
            x_copy.start()

    @pl.when(s != 0)
    def _():
        w_copy.wait()

    @pl.when(core == 0)
    def _():
        start_first()

    turn_weights(0, inner_turns)

    @pl.when(core == 1)
    def _():
        start_first()

    @pl.when(is_first)
    def _():
        turn(0, normal, 0)
        res_in(0).wait_send()

    @pl.when(s != 0)
    def _():
        turn_weights(inner_turns, pack // TURN)

    dy_copy.start()

    @pl.when(is_mixer)
    def _():
        begin = jnp.where(is_first, 1, 0)

        def forward(m, carry):
            @pl.when(m != s)
            def _():
                remote(mask_own, mask.at[m], mask_send.at[0], mask_recv.at[m], (0, d)).wait_recv()

            mixer_forward(m)

            @pl.when(m > begin)
            def _():
                res_in(m - 1).wait_send()

            res_in(m).start()
            turn(0, normal, m)
            return carry

        lax.fori_loop(begin, sections, forward, 0)

        def backward(m, carry):
            at = whole(m)
            x, q, _ = norm_in(m)
            grad_in(m).wait_recv()
            g_low = grad[at]
            d_normed = jnp.zeros((slot, width), F32)

            def project(c):
                return dot(g_low, w[:, 3 * gate + c : 3 * gate + c + BACK_CHUNK])

            for c, d_state in ahead_of(range(0, gate, BACK_CHUNK), project):
                adjoint = scan_up(stash[at, 3 * gate + c : 3 * gate + c + BACK_CHUNK], d_state)
                for k in range(3):
                    here = slice(k * gate + c, k * gate + c + BACK_CHUNK)
                    low = (adjoint * stash[at, here]).astype(BF16)
                    rows[at, here] = low
                    d_normed = d_normed + dot(low, wt[here, :])
            finish_back(m, x, q, d_normed)
            turn(1, grad, m)
            return carry

        lax.fori_loop(0, sections, backward, 0)

    @pl.when((lax.rem(s, 2) == 1) & (s != last))
    def _():
        def forward(m, carry):
            wait_res(m)
            at = whole(m)
            x, _, normed = norm_in(m)
            normal[at] = normed
            total = x

            def project(c):
                return dot(normed, w[:, c : c + DENSE_CHUNK])

            for c, hidden_in in ahead_of(range(0, ff, DENSE_CHUNK), project):
                hidden, bend = gelu_parts(hidden_in)
                low = hidden.astype(BF16)
                total = total + dot(low, wt[ff + c : ff + c + DENSE_CHUNK, :])
                rows[at, ff + c : ff + c + DENSE_CHUNK] = low
                stash[at, c : c + DENSE_CHUNK] = bend
            out[at] = total.astype(BF16)

            @pl.when(m > 0)
            def _():
                res_in(m - 1).wait_send()

            res_in(m).start()
            turn(0, normal, m)
            return carry

        lax.fori_loop(0, sections, forward, 0)

        def backward(m, carry):
            at = whole(m)
            x, q, _ = norm_in(m)
            grad_in(m).wait_recv()
            g_low = grad[at]
            d_normed = jnp.zeros((slot, width), F32)

            def project(c):
                return dot(g_low, w[:, ff + c : ff + c + DENSE_CHUNK])

            for c, d_act in ahead_of(range(0, ff, DENSE_CHUNK), project):
                low = (d_act * stash[at, c : c + DENSE_CHUNK]).astype(BF16)
                rows[at, c : c + DENSE_CHUNK] = low
                d_normed = d_normed + dot(low, wt[c : c + DENSE_CHUNK, :])
            finish_back(m, x, q, d_normed)
            turn(1, grad, m)
            return carry

        lax.fori_loop(0, sections, backward, 0)

    @pl.when(is_last)
    def _():
        def prepare(k, carry):
            m = last - k
            grad_in(m).wait_recv()
            at = whole(m)
            g_low = grad[at]
            for c in range(0, ff, DENSE_CHUNK):
                stash[at, c : c + DENSE_CHUNK] = dot(g_low, w[:, ff + c : ff + c + DENSE_CHUNK])
            turn(1, grad, m)
            return carry

        lax.fori_loop(0, sections, prepare, 0)

        def both(m, carry):
            wait_res(m)
            at = whole(m)
            x, q, normed = norm_in(m)
            normal[at] = normed
            d_normed = jnp.zeros((slot, width), F32)

            def project(c):
                return dot(normed, w[:, c : c + LAST_CHUNK])

            for c, hidden_in in ahead_of(range(0, ff, LAST_CHUNK), project):
                hidden, bend = gelu_parts(hidden_in)
                rows[at, ff + c : ff + c + LAST_CHUNK] = hidden.astype(BF16)
                low = (stash[at, c : c + LAST_CHUNK] * bend).astype(BF16)
                rows[at, c : c + LAST_CHUNK] = low
                d_normed = d_normed + dot(low, wt[c : c + LAST_CHUNK, :])
            finish_back(m, x, q, d_normed)
            turn(0, normal, m)
            return carry

        lax.fori_loop(0, sections, both, 0)

    @pl.when(is_mixer)
    def _():
        small[1:2, 0:GATE_CHUNK] = jnp.sum(forget_acc[...], axis=0, keepdims=True)
        used = mask[0, 1:2]
        for m in range(1, sections):
            used = used + mask[m, 1:2]
        small[2:3, 0:slot] = used

    split = jnp.where(is_mixer, 3 * gate, ff)

    def rows_at(k):
        return pl.ds(pl.multiple_of(lax.rem(k, stacked) * piece_rows, piece_rows), piece_rows)

    def cols_at(k, part_of):
        return pl.ds(pl.multiple_of(part_of * half + k // stacked * piece, piece), piece)

    def grad_piece(k, part_of):
        side = jnp.where(part_of * half + k // stacked * piece < split, 0, 1)
        return dot(left[side, rows_at(k)], rows[:, cols_at(k, part_of)])

    def sib_copy(k):
        return remote(sib_out.at[k], sib_in.at[k], sib_send, sib_recv.at[k], sibling)

    def inward(k):
        return remote(part.at[k], outer_in.at[k], part_send, outer_recv.at[k], inner)

    def across(k):
        return remote(part.at[k], tot_in.at[k], part_send, tot_recv.at[k], inner)

    def outward(k):
        return remote(tot_in.at[k], tot_in.at[k], tot_send, tot_recv.at[k], outer)

    def lend(k):
        return remote(part.at[2 * k + 1], guest_in.at[k], part_send, guest_recv.at[k], (host, d))

    def give_back(k):
        return remote(tot_in.at[pieces + k], tot_in.at[2 * k + 1], back_send, tot_recv.at[2 * k + 1], (giver, d))

    def final(k):
        return remote(
            tot_in.at[k], dw_ref.at[rows_at(k), cols_at(k, core)], fin_send, fin_recv, sibling
        )

    small_swap = remote(small, small_sib, small_send.at[0], small_recv.at[0], sibling)
    small_inward = remote(small_part, small_outer, small_send.at[1], small_recv.at[1], inner)
    small_across = remote(small_part, small_tot, small_send.at[1], small_recv.at[2], inner)
    small_outward = remote(small_tot, small_tot, small_send.at[2], small_recv.at[2], outer)

    def to_sibling(k):
        sib_out[k] = grad_piece(k, 1 - core).astype(BF16)
        sib_copy(k).start()

    to_sibling(0)
    small_swap.start()

    def reduce_small():
        small_swap.wait_recv()

        @pl.when(is_end)
        def _():
            small_part[...] = small[...] + small_sib[...]

        @pl.when(jnp.logical_not(is_end))
        def _():
            small_inward.wait_recv()
            small_part[...] = small[...] + small_sib[...] + small_outer[...]

        @pl.when(is_middle)
        def _():
            small_across.start()

        @pl.when(jnp.logical_not(is_middle))
        def _():
            small_inward.start()

    def far_copy(k):
        return remote(
            small_tot, small_far.at[s // 2], far_send.at[k - 1], far_recv.at[s // 2], (lax.rem(s + k, sections), other)
        )

    def total_small():
        small_across.wait_recv()

        @pl.when(is_middle)
        def _():
            small_tot[...] = small_tot[...] + small_part[...]

        @pl.when(jnp.logical_not(is_end))
        def _():
            small_outward.start()

        @pl.when(is_mixer)
        def _():
            small_far[s // 2] = small_tot[...]
            for k in range(1, sections):
                far_copy(k).start()

    def is_lent(k):
        return (s == giver) & (k < 2 * guests) & (lax.rem(k, 2) == 1)

    def reduce_piece(k):
        @pl.when(k < pieces)
        def _():
            work[...] = grad_piece(k, core)
            sib_copy(k).wait_recv()
            work[...] += sib_in[k].astype(F32)

        @pl.when(k >= pieces)
        def _():
            lend(k - pieces).wait_recv()
            work[...] = guest_in[k - pieces].astype(F32)

        on_line = jnp.logical_not(is_lent(k))

        @pl.when(is_lent(k) | is_end)
        def _():
            part[k] = work[...].astype(BF16)

        @pl.when(on_line & jnp.logical_not(is_end))
        def _():
            inward(k).wait_recv()
            part[k] = (work[...] + outer_in[k].astype(F32)).astype(BF16)

        @pl.when(is_lent(k))
        def _():
            lend(k // 2).start()

        @pl.when(on_line & is_middle)
        def _():
            across(k).start()

        @pl.when(on_line & jnp.logical_not(is_middle))
        def _():
            inward(k).start()

    def total_piece(k):
        across(k).wait_recv()
        on_line = jnp.logical_not(is_lent(k))

        @pl.when(on_line & is_middle)
        def _():
            tot_in[k] = (tot_in[k].astype(F32) + part[k].astype(F32)).astype(BF16)

        @pl.when(on_line & jnp.logical_not(is_end))
        def _():
            outward(k).start()

        @pl.when(k < pieces)
        def _():
            final(k).start()
            dw_ref[rows_at(k), cols_at(k, core)] = tot_in[k]

        @pl.when(k >= pieces)
        def _():
            give_back(k - pieces).start()

    on_list = pieces + jnp.where(s == host, guests, 0)
    lent = jnp.where(s == giver, guests, 0)
    lag = jnp.where(is_middle, lent + LAG, on_list)

    def in_order(p):
        return jnp.where(
            p < lent, 2 * p, jnp.where(p < on_list - lent, p + lent, 2 * (p - (on_list - lent)) + 1)
        )

    def step(i, carry):
        @pl.when(i + 1 < pieces)
        def _():
            to_sibling(i + 1)

        @pl.when(i < on_list)
        def _():
            reduce_piece(i)

        @pl.when(i == SMALL_STEP)
        def _():
            reduce_small()

        @pl.when(i == lag + SMALL_STEP)
        def _():
            total_small()

        @pl.when(i >= lag)
        def _():
            total_piece(jnp.where(s == giver, in_order(i - lag), i - lag))

        return carry

    lax.fori_loop(0, on_list + lag, step, 0)

    for k in range(sections // 2):

        @pl.when(s != 2 * k)
        def _():
            remote(small_tot, small_far.at[k], far_send.at[0], far_recv.at[k], sibling).wait_recv()

    dgain_ref[...] = small_tot[0:1, :]
    lanes = lax.broadcasted_iota(jnp.int32, (1, LANES), 1)
    means = jnp.zeros((1, LANES), F32)
    for k in range(sections // 2):
        sums = jnp.sum(small_far[k], axis=1, keepdims=True)
        means = jnp.where(lanes == k, sums[1:2] / (sums[2:3] * gate), means)
    fmean_ref[...] = means

    @pl.when(s != 0)
    def _():
        home(0, s).wait_recv()
        x_copy.wait_send()
        grad_in(last).wait_send()

    @pl.when(is_first)
    def _():
        for m in range(1, sections):
            grad_in(m).wait_send()

    dy_copy.wait_send()

    for k in range(sections // 2):

        @pl.when(s != 2 * k)
        def _():
            mask_copies[k].wait_send()

    @pl.when(s != last)
    def _():
        res_in(last).wait_send()

    small_swap.wait_send()
    small_across.wait_send()

    @pl.when(jnp.logical_not(is_end))
    def _():
        small_outward.wait_send()

    @pl.when(is_mixer)
    def _():
        for k in range(1, sections):
            far_copy(k).wait_send()

    remote(sib_out, sib_in, sib_send, sib_recv.at[0], sibling).wait_send()

    def sent(source, sem, n):
        remote(source.at[pl.ds(0, n)], source.at[pl.ds(0, n)], sem, sib_recv.at[0], sibling).wait_send()

    for n, holds in ((pieces - guests, s == giver), (pieces, (s != giver) & (s != host)), (pieces + guests, s == host)):

        @pl.when(holds & jnp.logical_not(is_end))
        def _():
            sent(tot_in, tot_send, n)

    @pl.when(s == host)
    def _():
        sent(part, part_send, pieces + guests)
        sent(guest_in, back_send, guests)

    @pl.when(s != host)
    def _():
        sent(part, part_send, pieces)

    sent(tot_in, fin_send, pieces)
    their_half = dw_ref.at[:, pl.ds(pl.multiple_of((1 - core) * half, half), half)]
    remote(their_half, their_half, fin_send, fin_recv, sibling).wait_recv()


def finish_kernel(dw_ref, ig_ref, dgain_ref, fmean_ref, ig_out, dw_out, dgain_out, fmean_out, wide_dw, sem):
    dgain_out[...] = dgain_ref[0]
    fmean_out[...] = fmean_ref[0, : fmean_out.shape[0]]
    slots, step = wide_dw.shape[:2]
    steps = dw_ref.shape[0] // step

    def copy(k):
        at = pl.ds(pl.multiple_of(k * step, step), step)
        return pltpu.make_async_copy(wide_dw.at[lax.rem(k, slots)], dw_out.at[at], sem.at[lax.rem(k, slots)])

    for k in range(steps):
        if k >= slots:
            copy(k - slots).wait()
        wide_dw[k % slots] = dw_ref[k * step : (k + 1) * step].astype(F32)
        copy(k).start()
    slot = ig_ref.shape[1]
    token_rows = lax.broadcasted_iota(jnp.int32, (slot, slot), 0)
    order = jnp.where(time_of_row(slot, (slot, slot), 1) == token_rows, 1.0, 0.0).astype(BF16)
    ig_out[0] = dot(order, ig_ref[0]).astype(BF16)
    for k in range(steps - slots, steps):
        copy(k).wait()


def finish(input_grad, weight_grads, gain_grads, means, sections):
    width, pack = weight_grads.shape
    vmem = pl.BlockSpec(memory_space=pltpu.VMEM)
    return pl.pallas_call(
        finish_kernel,
        out_shape=(
            jax.ShapeDtypeStruct(input_grad.shape, BF16),
            jax.ShapeDtypeStruct(weight_grads.shape, F32),
            jax.ShapeDtypeStruct((width,), F32),
            jax.ShapeDtypeStruct((sections // 2,), F32),
        ),
        in_specs=[vmem] * 4,
        out_specs=(vmem, pl.BlockSpec(memory_space=pl.ANY), vmem, vmem),
        scratch_shapes=[pltpu.VMEM((4, FINISH_ROWS, pack), F32), pltpu.SemaphoreType.DMA((4,))],
        compiler_params=pltpu.CompilerParams(vmem_limit_bytes=16 * 1024 * 1024),
    )(weight_grads, input_grad, gain_grads, means)


def local(count, inputs, cotangent, section_weights, norm_gains, doc_lengths, slot_fill):
    sections = lax.axis_size("section")
    slot, width = inputs.shape[1:]
    pack = section_weights.shape[1]
    gate, ff, half = pack // 4, pack // 2, pack // 2
    tokens = sections * slot
    pieces = half * width // (PIECE[0] * PIECE[1])
    dma = pltpu.SemaphoreType.DMA
    own = pltpu.VMEM((pieces, *PIECE), BF16)
    hosted = pltpu.VMEM((pieces + GUESTS, *PIECE), BF16)
    small = pltpu.VMEM((8, width), F32)
    stack = pltpu.VMEM((tokens, width), BF16)
    vmem = pl.BlockSpec(memory_space=pltpu.VMEM)
    anywhere = pl.BlockSpec(memory_space=pl.ANY)
    input_grad, weight_grads, gain_grads, means = pl.pallas_call(
        functools.partial(kernel, count),
        out_shape=(
            pltpu.VMEM((1, slot, width), BF16),
            pltpu.VMEM((width, pack), BF16),
            pltpu.VMEM((1, width), F32),
            pltpu.VMEM((1, LANES), F32),
        ),
        in_specs=[anywhere] * 6,
        out_specs=(vmem, vmem, vmem, vmem),
        scratch_shapes=[
            pltpu.VMEM((width, pack), BF16), pltpu.VMEM((pack, width), BF16),
            stack, stack, stack, stack, stack,
            pltpu.VMEM((slot, width), BF16), pltpu.VMEM((slot, width), BF16),
            pltpu.VMEM((sections, 8, slot), F32), pltpu.VMEM((8, slot), F32),
            pltpu.VMEM((slot, LANES), F32), pltpu.VMEM((slot, LANES), F32),
            pltpu.VMEM(inputs.shape, BF16), pltpu.VMEM(inputs.shape, BF16), pltpu.VMEM((1, width), F32),
            pltpu.SMEM(doc_lengths.shape, jnp.int32), pltpu.SMEM(slot_fill.shape, jnp.int32),
            pltpu.VMEM((tokens, pack), F32),
            pltpu.VMEM((tokens, pack), BF16),
            pltpu.VMEM((2, width, tokens), BF16),
            pltpu.VMEM((8, GATE_CHUNK), F32),
            own, own, hosted, hosted, hosted,
            pltpu.VMEM((GUESTS, *PIECE), BF16), pltpu.VMEM(PIECE, F32),
            small, small, small, small, small,
            pltpu.VMEM((sections // 2, 8, width), F32),
            dma, dma((5,)), dma, dma,
            dma((sections // 2,)),
            dma((sections,)), dma((sections,)), dma((sections,)), dma((sections,)),
            dma((sections,)), dma,
            dma, dma((pieces,)), dma, dma((pieces + GUESTS,)),
            dma, dma((pieces + GUESTS,)), dma, dma, dma((GUESTS,)), dma,
            dma((3,)), dma((3,)), dma((sections - 1,)), dma((sections // 2,)),
        ],
        compiler_params=pltpu.CompilerParams(
            collective_id=0, has_side_effects=True, vmem_limit_bytes=56 * 1024 * 1024
        ),
    )(inputs, cotangent, section_weights, norm_gains.reshape(1, width), doc_lengths, slot_fill)
    return finish(input_grad, weight_grads, gain_grads, means, sections)


def solution(mesh):
    placed = (
        P("section", "dp", None),
        P("section", "dp", None),
        P("section", None),
        P("section"),
        P("section", "dp", None),
        P("section", "dp"),
    )
    return jax.shard_map(
        functools.partial(local, mesh.shape["dp"]),
        mesh=mesh,
        in_specs=placed,
        out_specs=(P("section", "dp", None), P("section", None), P("section"), P()),
        check_vma=False,
    )
```

time: 133 us -> 115 us (0.86)
  Pallas kernels: 122 us -> 114 us
  other arithmetic: 6.7 us -> 0 us
  local copies, waits for them, and re-layouts: 2.36 us -> 0 us
    pallas_call x1 -> x2, Pallas kernels: 122 us -> 114 us  [the longest x1 109 us: local(): pl.pallas_call(functools.partial(kernel, count), out_shape=(pltpu.VMEM((1...]
    convert_element_type x1 -> x0, other arithmetic: 6.7 us -> none  [local(): weight_grads.astype(F32)]
where the time goes in v2:
time: 115 us
  Pallas kernels  114 us (99%)
  between operations  1.29 us (1%)
    pallas_call x1, Pallas kernels, local(): pl.pallas_call(functools.partial(kernel, count), out_shape=(pltpu.VMEM((1...  109 us
    pallas_call x1, Pallas kernels, finish(): pl.pallas_call(finish_kernel, out_shape=(jax.ShapeDtypeStruct(input_grad....  4.56 us

profile of v2, /device:TPU:0, one launch (start us, length us, event | category | flops | bytes accessed | tf_op | source)
XLA Modules:
  0.0 115.0 jit_solution(9779520500696327168)
XLA Ops:
  1.3 109.1 %shard_map.93 = (bf16[1,128,512]{2,1,0:T(8,128)(2,1)S(1)}, bf16[512,4096]{1,0:T(8,128)(2,1)S(1)}, f32[1,512]{1,0:T(1,128)S(1)}, f32[1,128]{1,0:T(1,128)S(1)}) custom-call(bf16[1,128,512]{2,1,0:T(8,128)(2,1)} %x_hbm.1, bf16[1,128,512]{2,1,0:T(8,128)(2,1)} %cot_hbm.1, bf16[512,4096]{1,0:T(8,128)(2,1)} %w_hbm.1, f32[1,512]{1,0:T(1,128)} %bitcast.1, ...), custom_call_target="tpu_custom_call" | custom-call | tf_op jit(solution)/shard_map/pallas_call | solution.py:817
  110.4 4.6 %shard_map.94 = (bf16[1,128,512]{2,1,0:T(8,128)(2,1)}, f32[512,4096]{1,0:T(8,128)}, f32[512]{0:T(512)}, f32[2]{0:T(128)}) custom-call(bf16[512,4096]{1,0:T(8,128)(2,1)S(1)} %get-tuple-element.8.dw_ref, bf16[1,128,512]{2,1,0:T(8,128)(2,1)S(1)} %get-tuple-element.9.ig_ref, f32[1,512]{1,0:T(1,128)S(1)} %get-tuple-element.10.dgain_ref, ...), custom_call_target="tpu_custom_call" | custom-call | tf_op jit(solution)/shard_map/pallas_call | solution.py:788

commit v3 on v2

--- a/solution.py
+++ b/solution.py
@@ -18,8 +18,14 @@
 LAST_CHUNK = 256
 TURN = 256
 PIECE = (256, 128)
-GUESTS = 5
-LAG = 3
+LENT = (7, 2)
+HOST_AT = 24
+SUB = 1
+LAG = 2
+STRIDE = 3
+AHEAD = 2
+SECOND_TURNS = 14
+FIRST_TURNS = 4
 SMALL_STEP = 3
 FINISH_ROWS = 32
 
@@ -99,11 +105,11 @@
     count,
     x_hbm, cot_hbm, w_hbm, gain_hbm, len_hbm, fill_hbm,
     ig_ref, dw_ref, dgain_ref, fmean_ref,
-    w, wt, res, grad, out, gout, normal, x_own, dy_own, mask, mask_own, keep_col, valid_col, x_ref, cot_ref, gain_ref, len_ref, fill_ref,
+    w, wt, res, grad, out, gout, normal, x_own, dy_own, mask, mask_own, keep_col, valid_col, relay, x_ref, cot_ref, gain_ref, len_ref, fill_ref,
     stash, rows, left, forget_acc,
     sib_out, sib_in, outer_in, part, tot_in, guest_in, work,
     small, small_sib, small_outer, small_part, small_tot, small_far,
-    w_sem, load_sem, x_send, dy_send, mask_send, res_send, res_recv, grad_send, grad_recv, mask_recv, ig_recv,
+    w_sem, load_sem, x_send, dy_send, mask_send, res_send, res_recv, grad_send, grad_recv, mask_recv, ig_recv, relay_send, relay_recv, turn_sem,
     sib_send, sib_recv, part_send, outer_recv, tot_send, tot_recv, fin_send, fin_recv, guest_recv, back_send,
     small_send, small_recv, far_send, far_recv,
 ):
@@ -119,11 +125,13 @@
     ff = pack // 2
     half = pack // 2
     pieces = sib_in.shape[0]
-    guests = guest_in.shape[0]
     piece_rows, piece = sib_in.shape[1:]
     stacked = width // piece_rows
     last = sections - 1
-    giver, host = 0, last
+    partner = last - s
+    lent = jnp.where(s == 0, LENT[0], jnp.where(s == 1, LENT[1], 0))
+    hosted = jnp.where(partner == 0, LENT[0], jnp.where(partner == 1, LENT[1], 0))
+    mine = lax.rem(core + chip, 2)
     is_first = s == 0
     is_last = s == last
     is_mixer = lax.rem(s, 2) == 0
@@ -132,8 +140,8 @@
     is_end = (chip == 0) | (chip == chips - 1)
     other = d + 1 - 2 * core
     sibling = (s, other)
-    inner = (s, jnp.where(on_left, d + 2, d - 2))
-    outer = (s, jnp.where(on_left, d - 2, d + 2))
+    inner = (s, jnp.where(on_left, other + 2, other - 2))
+    outer = (s, jnp.where(on_left, other - 2, other + 2))
 
     loads = [
         pltpu.make_async_copy(src, dst, load_sem.at[k])
@@ -144,7 +152,11 @@
     w_copy = pltpu.make_async_copy(w_hbm, w, w_sem)
     for load in loads:
         load.start()
-    w_copy.start()
+    w_early = is_first | is_last | (core == 1)
+
+    @pl.when(w_early)
+    def _():
+        w_copy.start()
 
     barrier = pltpu.get_barrier_semaphore()
     for by in range(1, sections):
@@ -156,11 +168,11 @@
 
     @pl.when(chip > 0)
     def _():
-        pl.semaphore_signal(barrier, inc=1, device_id=(s, d - 2), device_id_type=MESH)
+        pl.semaphore_signal(barrier, inc=1, device_id=(s, other - 2), device_id_type=MESH)
 
     @pl.when(chip < chips - 1)
     def _():
-        pl.semaphore_signal(barrier, inc=1, device_id=(s, d + 2), device_id_type=MESH)
+        pl.semaphore_signal(barrier, inc=1, device_id=(s, other + 2), device_id_type=MESH)
 
     def remote(src, dst, send, recv, target):
         return pltpu.make_async_remote_copy(
@@ -211,10 +223,6 @@
             res_in(m).wait_recv()
 
     def send_grad(m):
-        @pl.when((s != 0) & (m > 0))
-        def _():
-            grad_in(m - 1).wait_send()
-
         @pl.when(s != 0)
         def _():
             grad_in(m).start()
@@ -252,7 +260,7 @@
 
     gain = gain_ref[...]
 
-    def mixer_forward(m):
+    def mixer_forward(m, halfway=None):
         at = whole(m)
         masks = mask[m]
         keep_col[...] = jnp.broadcast_to(jnp.sum(order * masks[0:1], axis=1, keepdims=True), (slot, LANES))
@@ -285,6 +293,8 @@
             total = total + dot(state_low, wt[3 * gate + c : 3 * gate + c + GATE_CHUNK, :])
             rows[at, 3 * gate + c : 3 * gate + c + GATE_CHUNK] = state_low
             bend = soft - keep * previous
+            if halfway is not None and c == gate // 4:
+                halfway()
             stash[at, c : c + GATE_CHUNK] = -forget * (e_f * inv) * bend
             stash[at, gate + c : gate + c + GATE_CHUNK] = intake * (e_i * inv) * bend
             stash[at, 2 * gate + c : 2 * gate + c + GATE_CHUNK] = (
@@ -316,6 +326,8 @@
     dy_copy = remote(
         dy_own, grad.at[whole(s)], dy_send, grad_recv.at[s], (last, jnp.where(last % 2 == 1, other, d))
     )
+    dy_relayed = remote(dy_own, relay, dy_send, relay_recv, (2, d))
+    dy_onward = remote(relay, grad.at[whole(0)], relay_send, grad_recv.at[0], (last, other))
     mask_copies = [
         remote(mask_own, mask.at[s], mask_send.at[k], mask_recv.at[s], (2 * k, d))
         for k in range(sections // 2)
@@ -331,43 +343,58 @@
         def _():
             mask_copies[k].start()
 
-    def start_first():
-        @pl.when(is_first)
+    @pl.when(jnp.logical_not(w_early))
+    def _():
+        x_copy.start()
+        x_copy.wait_send()
+        w_copy.start()
+
+    @pl.when(s != 0)
+    def _():
+        w_copy.wait()
+        turn_weights(0, SECOND_TURNS)
+
+        @pl.when((s != last) & (core == 1))
+        def _():
+            x_copy.start()
+
+        turn_weights(SECOND_TURNS, pack // TURN)
+
+        @pl.when(s == last)
+        def _():
+            x_copy.start()
+
+    @pl.when(is_first)
+    def _():
+        @pl.when(core == 0)
         def _():
             res_in(0).start()
 
-        @pl.when(s != 0)
-        def _():
-            x_copy.start()
+        dy_relayed.start()
+        turn_weights(0, FIRST_TURNS)
+
+        @pl.when(core == 1)
+        def _():
+            res_in(0).start()
+
+        turn(0, normal, 0)
+
+    def give_turn():
+        pl.semaphore_signal(turn_sem, inc=1, device_id=sibling, device_id_type=MESH)
+
+    def take_turn():
+        pl.semaphore_wait(turn_sem, 1)
 
     @pl.when(s != 0)
     def _():
-        w_copy.wait()
-
-    @pl.when(core == 0)
-    def _():
-        start_first()
-
-    turn_weights(0, inner_turns)
-
-    @pl.when(core == 1)
-    def _():
-        start_first()
-
-    @pl.when(is_first)
-    def _():
-        turn(0, normal, 0)
-        res_in(0).wait_send()
-
-    @pl.when(s != 0)
-    def _():
-        turn_weights(inner_turns, pack // TURN)
-
-    dy_copy.start()
+        dy_copy.start()
 
     @pl.when(is_mixer)
     def _():
-        begin = jnp.where(is_first, 1, 0)
+        @pl.when(s == 2)
+        def _():
+            dy_relayed.wait_recv()
+            dy_onward.start()
 
         def forward(m, carry):
             @pl.when(m != s)
@@ -376,15 +403,32 @@
 
             mixer_forward(m)
 
-            @pl.when(m > begin)
+            @pl.when(is_first & (core == 1))
             def _():
-                res_in(m - 1).wait_send()
+                take_turn()
 
             res_in(m).start()
             turn(0, normal, m)
             return carry
 
-        lax.fori_loop(begin, sections, forward, 0)
+        lax.fori_loop(jnp.where(is_first, 1, 0), jnp.where(is_first, 2, sections), forward, 0)
+
+        @pl.when(is_first)
+        def _():
+            def by_turns(m, carry):
+                remote(mask_own, mask.at[m], mask_send.at[0], mask_recv.at[m], (0, d)).wait_recv()
+                mixer_forward(m, give_turn)
+                take_turn()
+                res_in(m).start()
+                turn(0, normal, m)
+                return carry
+
+            lax.fori_loop(2, sections, by_turns, 0)
+            turn_weights(FIRST_TURNS, inner_turns)
+
+            @pl.when(core == 0)
+            def _():
+                give_turn()
 
         def backward(m, carry):
             at = whole(m)
@@ -429,10 +473,6 @@
                 stash[at, c : c + DENSE_CHUNK] = bend
             out[at] = total.astype(BF16)
 
-            @pl.when(m > 0)
-            def _():
-                res_in(m - 1).wait_send()
-
             res_in(m).start()
             turn(0, normal, m)
             return carry
@@ -518,25 +558,36 @@
     def sib_copy(k):
         return remote(sib_out.at[k], sib_in.at[k], sib_send, sib_recv.at[k], sibling)
 
-    def inward(k):
-        return remote(part.at[k], outer_in.at[k], part_send, outer_recv.at[k], inner)
-
-    def across(k):
-        return remote(part.at[k], tot_in.at[k], part_send, tot_recv.at[k], inner)
-
-    def outward(k):
-        return remote(tot_in.at[k], tot_in.at[k], tot_send, tot_recv.at[k], outer)
+    sub_rows = piece_rows // SUB
+
+    def sub(buffer, k, q):
+        return buffer.at[k, q * sub_rows : (q + 1) * sub_rows]
+
+    def sub_at(k, q):
+        first = lax.rem(k, stacked) * piece_rows + q * sub_rows
+        return pl.ds(pl.multiple_of(first, sub_rows), sub_rows)
+
+    def inward(k, q):
+        return remote(sub(part, k, q), sub(outer_in, k, q), part_send, outer_recv.at[k * SUB + q], inner)
+
+    def across(k, q):
+        return remote(sub(part, k, q), sub(tot_in, k, q), part_send, tot_recv.at[k * SUB + q], inner)
+
+    def outward(k, q):
+        return remote(sub(tot_in, k, q), sub(tot_in, k, q), tot_send, tot_recv.at[k * SUB + q], outer)
+
+    def lent_piece(j):
+        return STRIDE * j + STRIDE - 1
 
     def lend(k):
-        return remote(part.at[2 * k + 1], guest_in.at[k], part_send, guest_recv.at[k], (host, d))
-
-    def give_back(k):
-        return remote(tot_in.at[pieces + k], tot_in.at[2 * k + 1], back_send, tot_recv.at[2 * k + 1], (giver, d))
-
-    def final(k):
-        return remote(
-            tot_in.at[k], dw_ref.at[rows_at(k), cols_at(k, core)], fin_send, fin_recv, sibling
-        )
+        return remote(part.at[lent_piece(k)], guest_in.at[k], part_send, guest_recv.at[k], (partner, d))
+
+    def give_back(k, q):
+        to = lent_piece(k - pieces)
+        return remote(sub(tot_in, k, q), sub(tot_in, to, q), back_send, tot_recv.at[to * SUB + q], (partner, d))
+
+    def final(k, q):
+        return remote(sub(tot_in, k, q), dw_ref.at[sub_at(k, q), cols_at(k, mine)], fin_send, fin_recv, sibling)
 
     small_swap = remote(small, small_sib, small_send.at[0], small_recv.at[0], sibling)
     small_inward = remote(small_part, small_outer, small_send.at[1], small_recv.at[1], inner)
@@ -544,10 +595,11 @@
     small_outward = remote(small_tot, small_tot, small_send.at[2], small_recv.at[2], outer)
 
     def to_sibling(k):
-        sib_out[k] = grad_piece(k, 1 - core).astype(BF16)
+        sib_out[k] = grad_piece(k, 1 - mine).astype(BF16)
         sib_copy(k).start()
 
-    to_sibling(0)
+    for k in range(AHEAD):
+        to_sibling(k)
     small_swap.start()
 
     def reduce_small():
@@ -593,12 +645,12 @@
                 far_copy(k).start()
 
     def is_lent(k):
-        return (s == giver) & (k < 2 * guests) & (lax.rem(k, 2) == 1)
+        return (k < STRIDE * lent) & (lax.rem(k, STRIDE) == STRIDE - 1)
 
     def reduce_piece(k):
         @pl.when(k < pieces)
         def _():
-            work[...] = grad_piece(k, core)
+            work[...] = grad_piece(k, mine)
             sib_copy(k).wait_recv()
             work[...] += sib_in[k].astype(F32)
 
@@ -609,81 +661,115 @@
 
         on_line = jnp.logical_not(is_lent(k))
 
-        @pl.when(is_lent(k) | is_end)
+        def pass_on(has_outer, send):
+            if not has_outer:
+                part[k] = work[...].astype(BF16)
+            for q in range(SUB):
+                if has_outer:
+                    inward(k, q).wait_recv()
+                    here = slice(q * sub_rows, (q + 1) * sub_rows)
+                    part[k, here] = (work[here] + outer_in[k, here].astype(F32)).astype(BF16)
+                send(k, q).start()
+
+        @pl.when(is_lent(k))
         def _():
             part[k] = work[...].astype(BF16)
-
-        @pl.when(on_line & jnp.logical_not(is_end))
-        def _():
-            inward(k).wait_recv()
-            part[k] = (work[...] + outer_in[k].astype(F32)).astype(BF16)
-
-        @pl.when(is_lent(k))
-        def _():
-            lend(k // 2).start()
+            lend(k // STRIDE).start()
 
         @pl.when(on_line & is_middle)
         def _():
-            across(k).start()
-
-        @pl.when(on_line & jnp.logical_not(is_middle))
-        def _():
-            inward(k).start()
+            pass_on(chips > 2, across)
+
+        if chips > 2:
+
+            @pl.when(on_line & is_end)
+            def _():
+                pass_on(False, inward)
+
+        if chips > 4:
+
+            @pl.when(on_line & jnp.logical_not(is_end | is_middle))
+            def _():
+                pass_on(True, inward)
 
     def total_piece(k):
-        across(k).wait_recv()
         on_line = jnp.logical_not(is_lent(k))
-
-        @pl.when(on_line & is_middle)
-        def _():
-            tot_in[k] = (tot_in[k].astype(F32) + part[k].astype(F32)).astype(BF16)
-
-        @pl.when(on_line & jnp.logical_not(is_end))
-        def _():
-            outward(k).start()
+        for q in range(SUB):
+            here = slice(q * sub_rows, (q + 1) * sub_rows)
+            across(k, q).wait_recv()
+
+            @pl.when(on_line & is_middle)
+            def _():
+                tot_in[k, here] = (tot_in[k, here].astype(F32) + part[k, here].astype(F32)).astype(BF16)
+
+            @pl.when(on_line & jnp.logical_not(is_end))
+            def _():
+                outward(k, q).start()
+
+            @pl.when(k < pieces)
+            def _():
+                final(k, q).start()
+
+            @pl.when(k >= pieces)
+            def _():
+                give_back(k, q).start()
 
         @pl.when(k < pieces)
         def _():
-            final(k).start()
-            dw_ref[rows_at(k), cols_at(k, core)] = tot_in[k]
-
-        @pl.when(k >= pieces)
-        def _():
-            give_back(k - pieces).start()
-
-    on_list = pieces + jnp.where(s == host, guests, 0)
-    lent = jnp.where(s == giver, guests, 0)
-    lag = jnp.where(is_middle, lent + LAG, on_list)
+            dw_ref[rows_at(k), cols_at(k, mine)] = tot_in[k]
+
+    on_list = pieces + hosted
+    on_line = on_list - lent
+    late = on_line - LAG
+
+    def listed(i):
+        return jnp.where(
+            i < HOST_AT, i, jnp.where(i < HOST_AT + hosted, i - HOST_AT + pieces, i - hosted)
+        )
+
+    def line_place(i):
+        return jnp.where(i < STRIDE * lent, i // STRIDE * (STRIDE - 1) + lax.rem(i, STRIDE), i - lent)
+
+    def of_line(r):
+        few = STRIDE - 1
+        return listed(jnp.where(r < few * lent, r // few * STRIDE + lax.rem(r, few), r + lent))
 
     def in_order(p):
         return jnp.where(
-            p < lent, 2 * p, jnp.where(p < on_list - lent, p + lent, 2 * (p - (on_list - lent)) + 1)
+            p < late, of_line(p), jnp.where(p < late + lent, lent_piece(p - late), of_line(p - lent))
         )
 
     def step(i, carry):
-        @pl.when(i + 1 < pieces)
-        def _():
-            to_sibling(i + 1)
-
-        @pl.when(i < on_list)
-        def _():
-            reduce_piece(i)
+        own = jnp.where(i < HOST_AT, i, i - hosted)
+        working = i < on_list
+
+        @pl.when((own + AHEAD < pieces) & ((i < HOST_AT) | (i >= HOST_AT + hosted)))
+        def _():
+            to_sibling(own + AHEAD)
+
+        @pl.when(working)
+        def _():
+            reduce_piece(listed(i))
 
         @pl.when(i == SMALL_STEP)
         def _():
             reduce_small()
 
-        @pl.when(i == lag + SMALL_STEP)
+        @pl.when(i == jnp.where(is_middle, 3 * SMALL_STEP, on_list + SMALL_STEP))
         def _():
             total_small()
 
-        @pl.when(i >= lag)
-        def _():
-            total_piece(jnp.where(s == giver, in_order(i - lag), i - lag))
+        place = line_place(i)
+        taken = is_middle & working & jnp.logical_not(is_lent(i)) & (place >= LAG)
+        at = jnp.where(working, place - LAG, jnp.where(is_middle, late, 0) + i - on_list)
+
+        @pl.when(taken | jnp.logical_not(working))
+        def _():
+            total_piece(in_order(at))
 
         return carry
 
-    lax.fori_loop(0, on_list + lag, step, 0)
+    lax.fori_loop(0, on_list + jnp.where(is_middle, LAG + lent, on_list), step, 0)
 
     for k in range(sections // 2):
 
@@ -702,15 +788,20 @@
     @pl.when(s != 0)
     def _():
         home(0, s).wait_recv()
+        grad_in(0).wait_send()
+
+    for m in range(1, sections):
+        grad_in(m).wait_send()
+
+    @pl.when(s == 2)
+    def _():
+        dy_onward.wait_send()
+
+    dy_copy.wait_send()
+
+    @pl.when(w_early & (s != 0))
+    def _():
         x_copy.wait_send()
-        grad_in(last).wait_send()
-
-    @pl.when(is_first)
-    def _():
-        for m in range(1, sections):
-            grad_in(m).wait_send()
-
-    dy_copy.wait_send()
 
     for k in range(sections // 2):
 
@@ -718,9 +809,11 @@
         def _():
             mask_copies[k].wait_send()
 
-    @pl.when(s != last)
-    def _():
-        res_in(last).wait_send()
+    for m in range(sections):
+
+        @pl.when(s != last)
+        def _():
+            res_in(m).wait_send()
 
     small_swap.wait_send()
     small_across.wait_send()
@@ -739,45 +832,59 @@
     def sent(source, sem, n):
         remote(source.at[pl.ds(0, n)], source.at[pl.ds(0, n)], sem, sib_recv.at[0], sibling).wait_send()
 
-    for n, holds in ((pieces - guests, s == giver), (pieces, (s != giver) & (s != host)), (pieces + guests, s == host)):
-
-        @pl.when(holds & jnp.logical_not(is_end))
-        def _():
-            sent(tot_in, tot_send, n)
-
-    @pl.when(s == host)
-    def _():
-        sent(part, part_send, pieces + guests)
-        sent(guest_in, back_send, guests)
-
-    @pl.when(s != host)
-    def _():
-        sent(part, part_send, pieces)
+    for q in range(sections):
+        given = LENT[q] if q < len(LENT) else 0
+        taken = LENT[last - q] if last - q < len(LENT) else 0
+
+        @pl.when((s == q) & jnp.logical_not(is_end))
+        def _():
+            sent(tot_in, tot_send, pieces - given + taken)
+
+        @pl.when(s == q)
+        def _():
+            sent(part, part_send, pieces + taken)
+            if taken:
+                sent(guest_in, back_send, taken)
 
     sent(tot_in, fin_send, pieces)
-    their_half = dw_ref.at[:, pl.ds(pl.multiple_of((1 - core) * half, half), half)]
+    their_half = dw_ref.at[:, pl.ds(pl.multiple_of((1 - mine) * half, half), half)]
     remote(their_half, their_half, fin_send, fin_recv, sibling).wait_recv()
 
 
-def finish_kernel(dw_ref, ig_ref, dgain_ref, fmean_ref, ig_out, dw_out, dgain_out, fmean_out, wide_dw, sem):
-    dgain_out[...] = dgain_ref[0]
-    fmean_out[...] = fmean_ref[0, : fmean_out.shape[0]]
+def finish_kernel(
+    dw_ref, ig_ref, dgain_ref, fmean_ref, ig_out, dw_out, dgain_out, fmean_out, wide_dw, ig, dgain, fmean, sem, small_sem
+):
     slots, step = wide_dw.shape[:2]
     steps = dw_ref.shape[0] // step
 
     def copy(k):
-        at = pl.ds(pl.multiple_of(k * step, step), step)
-        return pltpu.make_async_copy(wide_dw.at[lax.rem(k, slots)], dw_out.at[at], sem.at[lax.rem(k, slots)])
-
-    for k in range(steps):
-        if k >= slots:
-            copy(k - slots).wait()
+        return pltpu.make_async_copy(
+            wide_dw.at[k % slots], dw_out.at[pl.ds(k * step, step)], sem.at[k % slots]
+        )
+
+    def convert(k):
         wide_dw[k % slots] = dw_ref[k * step : (k + 1) * step].astype(F32)
         copy(k).start()
+
+    for k in range(slots):
+        convert(k)
     slot = ig_ref.shape[1]
     token_rows = lax.broadcasted_iota(jnp.int32, (slot, slot), 0)
     order = jnp.where(time_of_row(slot, (slot, slot), 1) == token_rows, 1.0, 0.0).astype(BF16)
-    ig_out[0] = dot(order, ig_ref[0]).astype(BF16)
+    ig[0] = dot(order, ig_ref[0]).astype(BF16)
+    dgain[...] = dgain_ref[0]
+    fmean[...] = fmean_ref[0, : fmean.shape[0]]
+    small = [
+        pltpu.make_async_copy(src, dst, small_sem.at[k])
+        for k, (src, dst) in enumerate(((ig, ig_out), (dgain, dgain_out), (fmean, fmean_out)))
+    ]
+    for one in small:
+        one.start()
+    for k in range(slots, steps):
+        copy(k - slots).wait()
+        convert(k)
+    for one in small:
+        one.wait()
     for k in range(steps - slots, steps):
         copy(k).wait()
 
@@ -785,6 +892,8 @@
 def finish(input_grad, weight_grads, gain_grads, means, sections):
     width, pack = weight_grads.shape
     vmem = pl.BlockSpec(memory_space=pltpu.VMEM)
+    anywhere = pl.BlockSpec(memory_space=pl.ANY)
+    slots = 8
     return pl.pallas_call(
         finish_kernel,
         out_shape=(
@@ -794,8 +903,15 @@
             jax.ShapeDtypeStruct((sections // 2,), F32),
         ),
         in_specs=[vmem] * 4,
-        out_specs=(vmem, pl.BlockSpec(memory_space=pl.ANY), vmem, vmem),
-        scratch_shapes=[pltpu.VMEM((4, FINISH_ROWS, pack), F32), pltpu.SemaphoreType.DMA((4,))],
+        out_specs=(anywhere,) * 4,
+        scratch_shapes=[
+            pltpu.VMEM((slots, FINISH_ROWS, pack), F32),
+            pltpu.VMEM(input_grad.shape, BF16),
+            pltpu.VMEM((width,), F32),
+            pltpu.VMEM((sections // 2,), F32),
+            pltpu.SemaphoreType.DMA((slots,)),
+            pltpu.SemaphoreType.DMA((3,)),
+        ],
         compiler_params=pltpu.CompilerParams(vmem_limit_bytes=16 * 1024 * 1024),
     )(weight_grads, input_grad, gain_grads, means)
 
@@ -809,7 +925,7 @@
     pieces = half * width // (PIECE[0] * PIECE[1])
     dma = pltpu.SemaphoreType.DMA
     own = pltpu.VMEM((pieces, *PIECE), BF16)
-    hosted = pltpu.VMEM((pieces + GUESTS, *PIECE), BF16)
+    hosted = pltpu.VMEM((pieces + max(LENT), *PIECE), BF16)
     small = pltpu.VMEM((8, width), F32)
     stack = pltpu.VMEM((tokens, width), BF16)
     vmem = pl.BlockSpec(memory_space=pltpu.VMEM)
@@ -830,6 +946,7 @@
             pltpu.VMEM((slot, width), BF16), pltpu.VMEM((slot, width), BF16),
             pltpu.VMEM((sections, 8, slot), F32), pltpu.VMEM((8, slot), F32),
             pltpu.VMEM((slot, LANES), F32), pltpu.VMEM((slot, LANES), F32),
+            pltpu.VMEM((slot, width), BF16),
             pltpu.VMEM(inputs.shape, BF16), pltpu.VMEM(inputs.shape, BF16), pltpu.VMEM((1, width), F32),
             pltpu.SMEM(doc_lengths.shape, jnp.int32), pltpu.SMEM(slot_fill.shape, jnp.int32),
             pltpu.VMEM((tokens, pack), F32),
@@ -837,15 +954,15 @@
             pltpu.VMEM((2, width, tokens), BF16),
             pltpu.VMEM((8, GATE_CHUNK), F32),
             own, own, hosted, hosted, hosted,
-            pltpu.VMEM((GUESTS, *PIECE), BF16), pltpu.VMEM(PIECE, F32),
+            pltpu.VMEM((max(LENT), *PIECE), BF16), pltpu.VMEM(PIECE, F32),
             small, small, small, small, small,
             pltpu.VMEM((sections // 2, 8, width), F32),
             dma, dma((5,)), dma, dma,
             dma((sections // 2,)),
             dma((sections,)), dma((sections,)), dma((sections,)), dma((sections,)),
-            dma((sections,)), dma,
-            dma, dma((pieces,)), dma, dma((pieces + GUESTS,)),
-            dma, dma((pieces + GUESTS,)), dma, dma, dma((GUESTS,)), dma,
+            dma((sections,)), dma, dma, dma, pltpu.SemaphoreType.REGULAR,
+            dma, dma((pieces,)), dma, dma(((pieces + max(LENT)) * SUB,)),
+            dma, dma(((pieces + max(LENT)) * SUB,)), dma, dma, dma((max(LENT),)), dma,
             dma((3,)), dma((3,)), dma((sections - 1,)), dma((sections // 2,)),
         ],
         compiler_params=pltpu.CompilerParams(

time: 115 us -> 106 us (0.922)
  Pallas kernels: 114 us -> 104 us
    pallas_call x1, Pallas kernels: 109 us -> 101 us  [local(): pl.pallas_call(functools.partial(kernel, count), out_shape=(pltpu.VMEM((1...]
where the time goes in v3:
time: 106 us; the launch traced here: 105 us
  Pallas kernels  104 us (98%)
  between operations  1.29 us (1%)
    pallas_call x1, Pallas kernels, local(): pl.pallas_call(functools.partial(kernel, count), out_shape=(pltpu.VMEM((1...  101 us
    pallas_call x1, Pallas kernels, finish(): pl.pallas_call(finish_kernel, out_shape=(jax.ShapeDtypeStruct(input_grad....  3.49 us

profile of v3, /device:TPU:0, one launch (start us, length us, event | category | flops | bytes accessed | tf_op | source)
XLA Modules:
  0.0 105.4 jit_solution(18014084837964355425)
XLA Ops:
  1.3 100.7 %shard_map.93 = (bf16[1,128,512]{2,1,0:T(8,128)(2,1)S(1)}, bf16[512,4096]{1,0:T(8,128)(2,1)S(1)}, f32[1,512]{1,0:T(1,128)S(1)}, f32[1,128]{1,0:T(1,128)S(1)}) custom-call(bf16[1,128,512]{2,1,0:T(8,128)(2,1)} %x_hbm.1, bf16[1,128,512]{2,1,0:T(8,128)(2,1)} %cot_hbm.1, bf16[512,4096]{1,0:T(8,128)(2,1)} %w_hbm.1, f32[1,512]{1,0:T(1,128)} %bitcast.1, ...), custom_call_target="tpu_custom_call" | custom-call | tf_op jit(solution)/shard_map/pallas_call | solution.py:933
  101.9 3.5 %shard_map.94 = (bf16[1,128,512]{2,1,0:T(8,128)(2,1)}, f32[512,4096]{1,0:T(8,128)}, f32[512]{0:T(512)}, f32[2]{0:T(128)}) custom-call(bf16[512,4096]{1,0:T(8,128)(2,1)S(1)} %get-tuple-element.8.dw_ref, bf16[1,128,512]{2,1,0:T(8,128)(2,1)S(1)} %get-tuple-element.9.ig_ref, f32[1,512]{1,0:T(1,128)S(1)} %get-tuple-element.10.dgain_ref, ...), custom_call_target="tpu_custom_call" | custom-call | tf_op jit(solution)/shard_map/pallas_call | solution.py:897

commit v4 on v3

--- a/solution.py
+++ b/solution.py
@@ -19,12 +19,13 @@
 TURN = 256
 PIECE = (256, 128)
 LENT = (7, 2)
-HOST_AT = 24
-SUB = 1
+HOST_AT = 26
+SUB = 2
+RING_PER_CHIP = 3
+SIB_RING = 6
 LAG = 2
 STRIDE = 3
-AHEAD = 2
-SECOND_TURNS = 14
+SECOND_TURNS = 10
 FIRST_TURNS = 4
 SMALL_STEP = 3
 FINISH_ROWS = 32
@@ -110,7 +111,7 @@
     sib_out, sib_in, outer_in, part, tot_in, guest_in, work,
     small, small_sib, small_outer, small_part, small_tot, small_far,
     w_sem, load_sem, x_send, dy_send, mask_send, res_send, res_recv, grad_send, grad_recv, mask_recv, ig_recv, relay_send, relay_recv, turn_sem,
-    sib_send, sib_recv, part_send, outer_recv, tot_send, tot_recv, fin_send, fin_recv, guest_recv, back_send,
+    sib_send, sib_recv, part_send, outer_recv, tot_send, tot_recv, fin_send, fin_recv, guest_recv, back_send, back_recv,
     small_send, small_recv, far_send, far_recv,
 ):
     s = lax.axis_index("section")
@@ -126,6 +127,7 @@
     half = pack // 2
     pieces = sib_in.shape[0]
     piece_rows, piece = sib_in.shape[1:]
+    ring = outer_recv.shape[0] // SUB
     stacked = width // piece_rows
     last = sections - 1
     partner = last - s
@@ -360,7 +362,7 @@
 
         turn_weights(SECOND_TURNS, pack // TURN)
 
-        @pl.when(s == last)
+        @pl.when(is_last & (core == 0))
         def _():
             x_copy.start()
 
@@ -509,6 +511,11 @@
             for c in range(0, ff, DENSE_CHUNK):
                 stash[at, c : c + DENSE_CHUNK] = dot(g_low, w[:, ff + c : ff + c + DENSE_CHUNK])
             turn(1, grad, m)
+
+            @pl.when((k == 0) & (core == 1))
+            def _():
+                x_copy.start()
+
             return carry
 
         lax.fori_loop(0, sections, prepare, 0)
@@ -556,7 +563,7 @@
         return dot(left[side, rows_at(k)], rows[:, cols_at(k, part_of)])
 
     def sib_copy(k):
-        return remote(sib_out.at[k], sib_in.at[k], sib_send, sib_recv.at[k], sibling)
+        return remote(sib_out.at[k], sib_in.at[k], sib_send, sib_recv.at[lax.rem(k, sib_recv.shape[0])], sibling)
 
     sub_rows = piece_rows // SUB
 
@@ -567,14 +574,17 @@
         first = lax.rem(k, stacked) * piece_rows + q * sub_rows
         return pl.ds(pl.multiple_of(first, sub_rows), sub_rows)
 
-    def inward(k, q):
-        return remote(sub(part, k, q), sub(outer_in, k, q), part_send, outer_recv.at[k * SUB + q], inner)
-
-    def across(k, q):
-        return remote(sub(part, k, q), sub(tot_in, k, q), part_send, tot_recv.at[k * SUB + q], inner)
-
-    def outward(k, q):
-        return remote(sub(tot_in, k, q), sub(tot_in, k, q), tot_send, tot_recv.at[k * SUB + q], outer)
+    def sem_at(r, q):
+        return lax.rem(r, ring) * SUB + q
+
+    def inward(k, r, q):
+        return remote(sub(part, k, q), sub(outer_in, k, q), part_send, outer_recv.at[sem_at(r, q)], inner)
+
+    def across(k, r, q):
+        return remote(sub(part, k, q), sub(tot_in, k, q), part_send, tot_recv.at[sem_at(r, q)], inner)
+
+    def outward(k, r, q):
+        return remote(sub(tot_in, k, q), sub(tot_in, k, q), tot_send, tot_recv.at[sem_at(r, q)], outer)
 
     def lent_piece(j):
         return STRIDE * j + STRIDE - 1
@@ -582,9 +592,8 @@
     def lend(k):
         return remote(part.at[lent_piece(k)], guest_in.at[k], part_send, guest_recv.at[k], (partner, d))
 
-    def give_back(k, q):
-        to = lent_piece(k - pieces)
-        return remote(sub(tot_in, k, q), sub(tot_in, to, q), back_send, tot_recv.at[to * SUB + q], (partner, d))
+    def give_back(j):
+        return remote(tot_in.at[pieces + j], tot_in.at[lent_piece(j)], back_send, back_recv.at[j], (partner, d))
 
     def final(k, q):
         return remote(sub(tot_in, k, q), dw_ref.at[sub_at(k, q), cols_at(k, mine)], fin_send, fin_recv, sibling)
@@ -598,8 +607,7 @@
         sib_out[k] = grad_piece(k, 1 - mine).astype(BF16)
         sib_copy(k).start()
 
-    for k in range(AHEAD):
-        to_sibling(k)
+    to_sibling(0)
     small_swap.start()
 
     def reduce_small():
@@ -647,7 +655,7 @@
     def is_lent(k):
         return (k < STRIDE * lent) & (lax.rem(k, STRIDE) == STRIDE - 1)
 
-    def reduce_piece(k):
+    def reduce_piece(k, r):
         @pl.when(k < pieces)
         def _():
             work[...] = grad_piece(k, mine)
@@ -666,10 +674,10 @@
                 part[k] = work[...].astype(BF16)
             for q in range(SUB):
                 if has_outer:
-                    inward(k, q).wait_recv()
+                    inward(k, r, q).wait_recv()
                     here = slice(q * sub_rows, (q + 1) * sub_rows)
                     part[k, here] = (work[here] + outer_in[k, here].astype(F32)).astype(BF16)
-                send(k, q).start()
+                send(k, r, q).start()
 
         @pl.when(is_lent(k))
         def _():
@@ -692,31 +700,38 @@
             def _():
                 pass_on(True, inward)
 
-    def total_piece(k):
-        on_line = jnp.logical_not(is_lent(k))
-        for q in range(SUB):
-            here = slice(q * sub_rows, (q + 1) * sub_rows)
-            across(k, q).wait_recv()
-
-            @pl.when(on_line & is_middle)
-            def _():
-                tot_in[k, here] = (tot_in[k, here].astype(F32) + part[k, here].astype(F32)).astype(BF16)
-
-            @pl.when(on_line & jnp.logical_not(is_end))
-            def _():
-                outward(k, q).start()
-
-            @pl.when(k < pieces)
-            def _():
+    def total_piece(k, r):
+        @pl.when(is_lent(k))
+        def _():
+            give_back(k // STRIDE).wait_recv()
+            for q in range(SUB):
                 final(k, q).start()
 
-            @pl.when(k >= pieces)
-            def _():
-                give_back(k, q).start()
+        @pl.when(jnp.logical_not(is_lent(k)))
+        def _():
+            for q in range(SUB):
+                here = slice(q * sub_rows, (q + 1) * sub_rows)
+                across(k, r, q).wait_recv()
+
+                @pl.when(is_middle)
+                def _():
+                    tot_in[k, here] = (tot_in[k, here].astype(F32) + part[k, here].astype(F32)).astype(BF16)
+
+                @pl.when(jnp.logical_not(is_end))
+                def _():
+                    outward(k, r, q).start()
+
+                @pl.when(k < pieces)
+                def _():
+                    final(k, q).start()
 
         @pl.when(k < pieces)
         def _():
             dw_ref[rows_at(k), cols_at(k, mine)] = tot_in[k]
+
+        @pl.when(k >= pieces)
+        def _():
+            give_back(k - pieces).start()
 
     on_list = pieces + hosted
     on_line = on_list - lent
@@ -735,21 +750,23 @@
         return listed(jnp.where(r < few * lent, r // few * STRIDE + lax.rem(r, few), r + lent))
 
     def in_order(p):
-        return jnp.where(
-            p < late, of_line(p), jnp.where(p < late + lent, lent_piece(p - late), of_line(p - lent))
-        )
+        r = jnp.where(p < late, p, p - lent)
+        return jnp.where((p >= late) & (p < late + lent), lent_piece(p - late), of_line(r)), r
+
+    lag = jnp.where(is_middle, LAG, jnp.minimum(ring - 2, on_line))
 
     def step(i, carry):
         own = jnp.where(i < HOST_AT, i, i - hosted)
         working = i < on_list
-
-        @pl.when((own + AHEAD < pieces) & ((i < HOST_AT) | (i >= HOST_AT + hosted)))
-        def _():
-            to_sibling(own + AHEAD)
+        place = line_place(i)
+
+        @pl.when((own + 1 < pieces) & ((i < HOST_AT) | (i >= HOST_AT + hosted)))
+        def _():
+            to_sibling(own + 1)
 
         @pl.when(working)
         def _():
-            reduce_piece(listed(i))
+            reduce_piece(listed(i), place)
 
         @pl.when(i == SMALL_STEP)
         def _():
@@ -759,17 +776,16 @@
         def _():
             total_small()
 
-        place = line_place(i)
-        taken = is_middle & working & jnp.logical_not(is_lent(i)) & (place >= LAG)
-        at = jnp.where(working, place - LAG, jnp.where(is_middle, late, 0) + i - on_list)
+        taken = working & jnp.logical_not(is_lent(i)) & (place >= lag)
+        at = jnp.where(working, place - lag, on_line - lag + i - on_list)
 
         @pl.when(taken | jnp.logical_not(working))
         def _():
-            total_piece(in_order(at))
+            total_piece(*in_order(at))
 
         return carry
 
-    lax.fori_loop(0, on_list + jnp.where(is_middle, LAG + lent, on_list), step, 0)
+    lax.fori_loop(0, on_list + lag + lent, step, 0)
 
     for k in range(sections // 2):
 
@@ -924,6 +940,7 @@
     tokens = sections * slot
     pieces = half * width // (PIECE[0] * PIECE[1])
     dma = pltpu.SemaphoreType.DMA
+    ring = min(pieces + max(LENT), RING_PER_CHIP * (count // 2))
     own = pltpu.VMEM((pieces, *PIECE), BF16)
     hosted = pltpu.VMEM((pieces + max(LENT), *PIECE), BF16)
     small = pltpu.VMEM((8, width), F32)
@@ -961,8 +978,8 @@
             dma((sections // 2,)),
             dma((sections,)), dma((sections,)), dma((sections,)), dma((sections,)),
             dma((sections,)), dma, dma, dma, pltpu.SemaphoreType.REGULAR,
-            dma, dma((pieces,)), dma, dma(((pieces + max(LENT)) * SUB,)),
-            dma, dma(((pieces + max(LENT)) * SUB,)), dma, dma, dma((max(LENT),)), dma,
+            dma, dma((SIB_RING,)), dma, dma((ring * SUB,)), dma, dma((ring * SUB,)),
+            dma, dma, dma((max(LENT),)), dma, dma((max(LENT),)),
             dma((3,)), dma((3,)), dma((sections - 1,)), dma((sections // 2,)),
         ],
         compiler_params=pltpu.CompilerParams(

time: 106 us -> 105 us (level)
  no operation moved by 1% of the time
where the time goes in v4:
time: 105 us
  Pallas kernels  104 us (99%)
  between operations  1.29 us (1%)
    pallas_call x1, Pallas kernels, local(): pl.pallas_call(functools.partial(kernel, count), out_shape=(pltpu.VMEM((1...  100 us
    pallas_call x1, Pallas kernels, finish(): pl.pallas_call(finish_kernel, out_shape=(jax.ShapeDtypeStruct(input_grad....  3.49 us

profile of v4, /device:TPU:0, one launch (start us, length us, event | category | flops | bytes accessed | tf_op | source)
XLA Modules:
  0.0 104.9 jit_solution(2266885510338020283)
XLA Ops:
  1.3 100.1 %shard_map.93 = (bf16[1,128,512]{2,1,0:T(8,128)(2,1)S(1)}, bf16[512,4096]{1,0:T(8,128)(2,1)S(1)}, f32[1,512]{1,0:T(1,128)S(1)}, f32[1,128]{1,0:T(1,128)S(1)}) custom-call(bf16[1,128,512]{2,1,0:T(8,128)(2,1)} %x_hbm.1, bf16[1,128,512]{2,1,0:T(8,128)(2,1)} %cot_hbm.1, bf16[512,4096]{1,0:T(8,128)(2,1)} %w_hbm.1, f32[1,512]{1,0:T(1,128)} %bitcast.1, ...), custom_call_target="tpu_custom_call" | custom-call | tf_op jit(solution)/shard_map/pallas_call | solution.py:950
  101.4 3.5 %shard_map.94 = (bf16[1,128,512]{2,1,0:T(8,128)(2,1)}, f32[512,4096]{1,0:T(8,128)}, f32[512]{0:T(512)}, f32[2]{0:T(128)}) custom-call(bf16[512,4096]{1,0:T(8,128)(2,1)S(1)} %get-tuple-element.8.dw_ref, bf16[1,128,512]{2,1,0:T(8,128)(2,1)S(1)} %get-tuple-element.9.ig_ref, f32[1,512]{1,0:T(1,128)S(1)} %get-tuple-element.10.dgain_ref, ...), custom_call_target="tpu_custom_call" | custom-call | tf_op jit(solution)/shard_map/pallas_call | solution.py:913

commit v5 on v4

--- a/solution.py
+++ b/solution.py
@@ -25,8 +25,8 @@
 SIB_RING = 6
 LAG = 2
 STRIDE = 3
-SECOND_TURNS = 10
-FIRST_TURNS = 4
+SECOND_TURNS = 5
+FIRST_TURNS = 1
 SMALL_STEP = 3
 FINISH_ROWS = 32
 
@@ -154,7 +154,7 @@
     w_copy = pltpu.make_async_copy(w_hbm, w, w_sem)
     for load in loads:
         load.start()
-    w_early = is_first | is_last | (core == 1)
+    w_early = is_first | is_last | (core == 0)
 
     @pl.when(w_early)
     def _():
@@ -217,7 +217,7 @@
         )
 
     def home(m, to):
-        return remote(gout.at[whole(m)], ig_ref.at[0], grad_send.at[m], ig_recv, (to, d))
+        return remote(gout.at[whole(m)], ig_ref.at[0], grad_send.at[m], ig_recv, (to, other))
 
     def wait_res(m):
         @pl.when((s != 0) | (m != 0))
@@ -278,17 +278,16 @@
             return [dot(normed, w[:, k * gate + c : k * gate + c + GATE_CHUNK]) for k in range(3)]
 
         for c, (f_in, i_in, c_in) in ahead_of(range(0, gate, GATE_CHUNK), project):
-            top = jnp.maximum(jnp.maximum(-f_in, -i_in), 0.0)
-            e_zero = jnp.exp(-top)
-            e_f = jnp.exp(-f_in - top)
-            e_i = jnp.exp(-i_in - top)
+            least = jnp.minimum(jnp.minimum(f_in, i_in), 0.0)
+            e_zero = jnp.exp(least)
+            e_f = jnp.exp(least - f_in)
+            e_i = jnp.exp(least - i_in)
             u_f = e_zero + e_f
             u_i = e_zero + e_i
             inv = 1.0 / (u_f + u_i)
             forget = u_i * inv
             intake = u_f * inv
-            e_c = jnp.exp(-jnp.abs(c_in))
-            soft = jnp.maximum(c_in, 0.0) + jnp.log1p(e_c)
+            soft = jnp.maximum(c_in, 0.0) + jnp.log1p(jnp.exp(-jnp.abs(c_in)))
             decay = forget * keep
             state, previous = scan_down(decay, intake * soft)
             state_low = state.astype(BF16)
@@ -299,9 +298,7 @@
                 halfway()
             stash[at, c : c + GATE_CHUNK] = -forget * (e_f * inv) * bend
             stash[at, gate + c : gate + c + GATE_CHUNK] = intake * (e_i * inv) * bend
-            stash[at, 2 * gate + c : 2 * gate + c + GATE_CHUNK] = (
-                intake * jnp.where(c_in >= 0.0, 1.0, e_c) / (1.0 + e_c)
-            )
+            stash[at, 2 * gate + c : 2 * gate + c + GATE_CHUNK] = intake * jnp.exp(c_in - soft)
             stash[at, 3 * gate + c : 3 * gate + c + GATE_CHUNK] = decay
             counted = forget * valid
             folded = counted[:8]
@@ -324,26 +321,26 @@
         barrier, 2 * sections - 1 + jnp.where(chip > 0, 1, 0) + jnp.where(chip < chips - 1, 1, 0)
     )
 
-    x_copy = remote(x_own, res.at[whole(s)], x_send, res_recv.at[s], (0, d))
+    x_copy = remote(x_own, res.at[whole(s)], x_send, res_recv.at[s], (0, other))
     dy_copy = remote(
-        dy_own, grad.at[whole(s)], dy_send, grad_recv.at[s], (last, jnp.where(last % 2 == 1, other, d))
+        dy_own, grad.at[whole(s)], dy_send, grad_recv.at[s], (last, d)
     )
     dy_relayed = remote(dy_own, relay, dy_send, relay_recv, (2, d))
     dy_onward = remote(relay, grad.at[whole(0)], relay_send, grad_recv.at[0], (last, other))
     mask_copies = [
-        remote(mask_own, mask.at[s], mask_send.at[k], mask_recv.at[s], (2 * k, d))
+        remote(mask_own, mask.at[s], mask_send.at[k], mask_recv.at[s], (2 * k, jnp.where(is_first, d, other)))
         for k in range(sections // 2)
     ]
 
     for k in range(sections // 2):
 
-        @pl.when((s == 2 * k) & (s != 0))
-        def _():
-            mask[s] = mask_own[...]
-
-        @pl.when(s != 2 * k)
+        @pl.when((s != 0) | (k != 0))
         def _():
             mask_copies[k].start()
+
+    @pl.when(is_last)
+    def _():
+        grad[whole(last)] = dy_own[...]
 
     @pl.when(jnp.logical_not(w_early))
     def _():
@@ -356,13 +353,13 @@
         w_copy.wait()
         turn_weights(0, SECOND_TURNS)
 
-        @pl.when((s != last) & (core == 1))
+        @pl.when((s != last) & (core == 0))
         def _():
             x_copy.start()
 
         turn_weights(SECOND_TURNS, pack // TURN)
 
-        @pl.when(is_last & (core == 0))
+        @pl.when(is_last & (core == 1))
         def _():
             x_copy.start()
 
@@ -387,7 +384,7 @@
     def take_turn():
         pl.semaphore_wait(turn_sem, 1)
 
-    @pl.when(s != 0)
+    @pl.when((s != 0) & (s != last))
     def _():
         dy_copy.start()
 
@@ -399,7 +396,7 @@
             dy_onward.start()
 
         def forward(m, carry):
-            @pl.when(m != s)
+            @pl.when((s != 0) | (m != 0))
             def _():
                 remote(mask_own, mask.at[m], mask_send.at[0], mask_recv.at[m], (0, d)).wait_recv()
 
@@ -505,14 +502,18 @@
     def _():
         def prepare(k, carry):
             m = last - k
-            grad_in(m).wait_recv()
+
+            @pl.when(m != last)
+            def _():
+                grad_in(m).wait_recv()
+
             at = whole(m)
             g_low = grad[at]
             for c in range(0, ff, DENSE_CHUNK):
                 stash[at, c : c + DENSE_CHUNK] = dot(g_low, w[:, ff + c : ff + c + DENSE_CHUNK])
             turn(1, grad, m)
 
-            @pl.when((k == 0) & (core == 1))
+            @pl.when((k == 0) & (core == 0))
             def _():
                 x_copy.start()
 
@@ -813,7 +814,9 @@
     def _():
         dy_onward.wait_send()
 
-    dy_copy.wait_send()
+    @pl.when(s != last)
+    def _():
+        dy_copy.wait_send()
 
     @pl.when(w_early & (s != 0))
     def _():
@@ -821,7 +824,7 @@
 
     for k in range(sections // 2):
 
-        @pl.when(s != 2 * k)
+        @pl.when((s != 0) | (k != 0))
         def _():
             mask_copies[k].wait_send()
 

time: 105 us -> 105 us (level)
  no operation moved by 1% of the time
where the time goes in v5:
time: 105 us; the launch traced here: 104 us
  Pallas kernels  103 us (98%)
  between operations  1.29 us (1%)
    pallas_call x1, Pallas kernels, local(): pl.pallas_call(functools.partial(kernel, count), out_shape=(pltpu.VMEM((1...  99.6 us
    pallas_call x1, Pallas kernels, finish(): pl.pallas_call(finish_kernel, out_shape=(jax.ShapeDtypeStruct(input_grad....  3.49 us

profile of v5, /device:TPU:0, one launch (start us, length us, event | category | flops | bytes accessed | tf_op | source)
XLA Modules:
  0.0 104.4 jit_solution(16035311323210882141)
XLA Ops:
  1.3 99.6 %shard_map.93 = (bf16[1,128,512]{2,1,0:T(8,128)(2,1)S(1)}, bf16[512,4096]{1,0:T(8,128)(2,1)S(1)}, f32[1,512]{1,0:T(1,128)S(1)}, f32[1,128]{1,0:T(1,128)S(1)}) custom-call(bf16[1,128,512]{2,1,0:T(8,128)(2,1)} %x_hbm.1, bf16[1,128,512]{2,1,0:T(8,128)(2,1)} %cot_hbm.1, bf16[512,4096]{1,0:T(8,128)(2,1)} %w_hbm.1, f32[1,512]{1,0:T(1,128)} %bitcast.1, ...), custom_call_target="tpu_custom_call" | custom-call | tf_op jit(solution)/shard_map/pallas_call | solution.py:953
  100.9 3.5 %shard_map.94 = (bf16[1,128,512]{2,1,0:T(8,128)(2,1)}, f32[512,4096]{1,0:T(8,128)}, f32[512]{0:T(512)}, f32[2]{0:T(128)}) custom-call(bf16[512,4096]{1,0:T(8,128)(2,1)S(1)} %get-tuple-element.8.dw_ref, bf16[1,128,512]{2,1,0:T(8,128)(2,1)S(1)} %get-tuple-element.9.ig_ref, f32[1,512]{1,0:T(1,128)S(1)} %get-tuple-element.10.dgain_ref, ...), custom_call_target="tpu_custom_call" | custom-call | tf_op jit(solution)/shard_map/pallas_call | solution.py:916

commit v6 on v5

--- a/solution.py
+++ b/solution.py
@@ -19,12 +19,12 @@
 TURN = 256
 PIECE = (256, 128)
 LENT = (7, 2)
-HOST_AT = 26
+HOST_AT = 23
 SUB = 2
 RING_PER_CHIP = 3
 SIB_RING = 6
 LAG = 2
-STRIDE = 3
+STRIDE = 2
 SECOND_TURNS = 5
 FIRST_TURNS = 1
 SMALL_STEP = 3

time: 105 us -> 104 us (level)
  no operation moved by 1% of the time
where the time goes in v6:
time: 104 us
  Pallas kernels  103 us (99%)
  between operations  1.29 us (1%)
    pallas_call x1, Pallas kernels, local(): pl.pallas_call(functools.partial(kernel, count), out_shape=(pltpu.VMEM((1...  99.4 us
    pallas_call x1, Pallas kernels, finish(): pl.pallas_call(finish_kernel, out_shape=(jax.ShapeDtypeStruct(input_grad....  3.49 us

profile of v6, /device:TPU:0, one launch (start us, length us, event | category | flops | bytes accessed | tf_op | source)
XLA Modules:
  0.0 104.2 jit_solution(9311761350511991759)
XLA Ops:
  1.3 99.4 %shard_map.93 = (bf16[1,128,512]{2,1,0:T(8,128)(2,1)S(1)}, bf16[512,4096]{1,0:T(8,128)(2,1)S(1)}, f32[1,512]{1,0:T(1,128)S(1)}, f32[1,128]{1,0:T(1,128)S(1)}) custom-call(bf16[1,128,512]{2,1,0:T(8,128)(2,1)} %x_hbm.1, bf16[1,128,512]{2,1,0:T(8,128)(2,1)} %cot_hbm.1, bf16[512,4096]{1,0:T(8,128)(2,1)} %w_hbm.1, f32[1,512]{1,0:T(1,128)} %bitcast.1, ...), custom_call_target="tpu_custom_call" | custom-call | tf_op jit(solution)/shard_map/pallas_call | solution.py:953
  100.7 3.5 %shard_map.94 = (bf16[1,128,512]{2,1,0:T(8,128)(2,1)}, f32[512,4096]{1,0:T(8,128)}, f32[512]{0:T(512)}, f32[2]{0:T(128)}) custom-call(bf16[512,4096]{1,0:T(8,128)(2,1)S(1)} %get-tuple-element.8.dw_ref, bf16[1,128,512]{2,1,0:T(8,128)(2,1)S(1)} %get-tuple-element.9.ig_ref, f32[1,512]{1,0:T(1,128)S(1)} %get-tuple-element.10.dgain_ref, ...), custom_call_target="tpu_custom_call" | custom-call | tf_op jit(solution)/shard_map/pallas_call | solution.py:916

commit v7 on v6

--- a/solution.py
+++ b/solution.py
@@ -208,16 +208,16 @@
 
     def res_in(m):
         return remote(
-            out.at[whole(m)], res.at[whole(m)], res_send.at[m], res_recv.at[m], (jnp.minimum(s + 1, last), other)
+            out.at[whole(m)], res.at[whole(m)], res_send, res_recv.at[m], (jnp.minimum(s + 1, last), other)
         )
 
     def grad_in(m):
         return remote(
-            gout.at[whole(m)], grad.at[whole(m)], grad_send.at[m], grad_recv.at[m], (jnp.maximum(s - 1, 0), other)
+            gout.at[whole(m)], grad.at[whole(m)], grad_send, grad_recv.at[m], (jnp.maximum(s - 1, 0), other)
         )
 
     def home(m, to):
-        return remote(gout.at[whole(m)], ig_ref.at[0], grad_send.at[m], ig_recv, (to, other))
+        return remote(gout.at[whole(m)], ig_ref.at[0], grad_send, ig_recv, (to, other))
 
     def wait_res(m):
         @pl.when((s != 0) | (m != 0))
@@ -805,10 +805,12 @@
     @pl.when(s != 0)
     def _():
         home(0, s).wait_recv()
-        grad_in(0).wait_send()
-
-    for m in range(1, sections):
-        grad_in(m).wait_send()
+        remote(gout, grad, grad_send, grad_recv.at[0], sibling).wait_send()
+
+    @pl.when(s == 0)
+    def _():
+        sent_home = gout.at[pl.ds(slot, tokens - slot)]
+        remote(sent_home, sent_home, grad_send, ig_recv, sibling).wait_send()
 
     @pl.when(s == 2)
     def _():
@@ -828,11 +830,9 @@
         def _():
             mask_copies[k].wait_send()
 
-    for m in range(sections):
-
-        @pl.when(s != last)
-        def _():
-            res_in(m).wait_send()
+    @pl.when(s != last)
+    def _():
+        remote(out, res, res_send, res_recv.at[0], sibling).wait_send()
 
     small_swap.wait_send()
     small_across.wait_send()
@@ -979,7 +979,7 @@
             pltpu.VMEM((sections // 2, 8, width), F32),
             dma, dma((5,)), dma, dma,
             dma((sections // 2,)),
-            dma((sections,)), dma((sections,)), dma((sections,)), dma((sections,)),
+            dma, dma((sections,)), dma, dma((sections,)),
             dma((sections,)), dma, dma, dma, pltpu.SemaphoreType.REGULAR,
             dma, dma((SIB_RING,)), dma, dma((ring * SUB,)), dma, dma((ring * SUB,)),
             dma, dma, dma((max(LENT),)), dma, dma((max(LENT),)),

time: 104 us -> 104 us (level)
  no operation moved by 1% of the time
where the time goes in v7:
time: 104 us
  Pallas kernels  103 us (99%)
  between operations  1.29 us (1%)
    pallas_call x1, Pallas kernels, local(): pl.pallas_call(functools.partial(kernel, count), out_shape=(pltpu.VMEM((1...  99.4 us
    pallas_call x1, Pallas kernels, finish(): pl.pallas_call(finish_kernel, out_shape=(jax.ShapeDtypeStruct(input_grad....  3.49 us

profile of v7, /device:TPU:0, one launch (start us, length us, event | category | flops | bytes accessed | tf_op | source)
XLA Modules:
  0.0 104.2 jit_solution(12194363499006191671)
XLA Ops:
  1.3 99.4 %shard_map.93 = (bf16[1,128,512]{2,1,0:T(8,128)(2,1)S(1)}, bf16[512,4096]{1,0:T(8,128)(2,1)S(1)}, f32[1,512]{1,0:T(1,128)S(1)}, f32[1,128]{1,0:T(1,128)S(1)}) custom-call(bf16[1,128,512]{2,1,0:T(8,128)(2,1)} %x_hbm.1, bf16[1,128,512]{2,1,0:T(8,128)(2,1)} %cot_hbm.1, bf16[512,4096]{1,0:T(8,128)(2,1)} %w_hbm.1, f32[1,512]{1,0:T(1,128)} %bitcast.1, ...), custom_call_target="tpu_custom_call" | custom-call | tf_op jit(solution)/shard_map/pallas_call | solution.py:953
  100.7 3.5 %shard_map.94 = (bf16[1,128,512]{2,1,0:T(8,128)(2,1)}, f32[512,4096]{1,0:T(8,128)}, f32[512]{0:T(512)}, f32[2]{0:T(128)}) custom-call(bf16[512,4096]{1,0:T(8,128)(2,1)S(1)} %get-tuple-element.8.dw_ref, bf16[1,128,512]{2,1,0:T(8,128)(2,1)S(1)} %get-tuple-element.9.ig_ref, f32[1,512]{1,0:T(1,128)S(1)} %get-tuple-element.10.dgain_ref, ...), custom_call_target="tpu_custom_call" | custom-call | tf_op jit(solution)/shard_map/pallas_call | solution.py:916
